TPU v7x, 32 devices: a whole 2x2x4 slice. The times are simulated.
32 devices in a mesh: dp: 8 (over y, x, core), blk: 4 (over z).
Axes of the slice: x: 2, y: 2, z: 4, core: 2. Of those that a mesh axis runs over, the one named last changes fastest.
Arguments:
- hidden_in: bfloat16 [2, 8, 1024, 768], P(None, 'dp', 'blk'), may hold values from -6 to 6
- segment_ids: int32 [2, 8, 1024], P(None, 'dp', 'blk'), may hold values from 0 to 15, as said below
- queries: bfloat16 [2, 128, 768], P(None, 'dp'), may hold values from -0.5390625 to 0.5390625
- targets: int32 [2, 128], P(None, 'dp'), may hold values from 0 to 127, each once within a row
- cotangent: bfloat16 [2, 8, 1024, 768], P(None, 'dp', 'blk'), may hold values from -3 to 3
- query_weight: bfloat16 [768, 768], P('dp'), may hold values from -0.21875 to 0.21875
- key_weight: bfloat16 [768, 768], P('dp'), may hold values from -0.21875 to 0.21875
- value_weight: bfloat16 [768, 768], P('dp'), may hold values from -0.21875 to 0.21875
- output_weight: bfloat16 [768, 768], P('dp'), may hold values from -1.75 to 1.75
- query_bias: bfloat16 [768], P('dp'), may hold values from -3 to 3
- value_bias: bfloat16 [768], P('dp'), may hold values from -0.29882812 to 0.29882812
- output_bias: bfloat16 [768], P('dp'), may hold values from -1.1953125 to 1.1953125
- first_gain: bfloat16 [768], P('dp'), may hold values from 0.5 to 1.5
- first_shift: bfloat16 [768], P('dp'), may hold values from -1.1953125 to 1.1953125
- inner_weight: bfloat16 [768, 3072], P('dp'), may hold values from -0.21875 to 0.21875
- inner_bias: bfloat16 [3072], P('dp'), may hold values from -1.796875 to 1.796875
- outer_weight: bfloat16 [3072, 768], P('dp'), may hold values from -0.109375 to 0.109375
- outer_bias: bfloat16 [768], P('dp'), may hold values from -1.1953125 to 1.1953125
- second_gain: bfloat16 [768], P('dp'), may hold values from 0.5 to 1.5
- second_shift: bfloat16 [768], P('dp'), may hold values from -1.1953125 to 1.1953125
Outputs:
- hidden_out: bfloat16 [2, 8, 1024, 768], P(None, 'dp', 'blk')
- embeddings: bfloat16 [2, 128, 768], P(None, 'dp')
- query_loss: float32 [2, 128], P(None, 'dp')
- query_grad: float32 [2, 128, 768], P(None, 'dp')
- hidden_grad: bfloat16 [2, 8, 1024, 768], P(None, 'dp', 'blk')
- query_weight_grad: float32 [768, 768], P('dp')
- key_weight_grad: float32 [768, 768], P('dp')
- value_weight_grad: float32 [768, 768], P('dp')
- output_weight_grad: float32 [768, 768], P('dp')
- query_bias_grad: float32 [768], P('dp')
- value_bias_grad: float32 [768], P('dp')
- output_bias_grad: float32 [768], P('dp')
- first_gain_grad: float32 [768], P('dp')
- first_shift_grad: float32 [768], P('dp')
- inner_weight_grad: float32 [768, 3072], P('dp')
- inner_bias_grad: float32 [3072], P('dp')
- outer_weight_grad: float32 [3072, 768], P('dp')
- outer_bias_grad: float32 [768], P('dp')
- second_gain_grad: float32 [768], P('dp')
- second_shift_grad: float32 [768], P('dp')
Inputs may be any that keep to these rules, and one draw needn't show every extreme that they name: `segment_ids`: in each row the segment numbers never fall along the row and every number occurs; the first position of a segment is its CLS token. For each index of dp, one of its rows in one of the micro-batches holds a segment that begins within the first 256 positions and ends within the last 256; in every other row each block of 256 positions holds the first positions of exactly 4 segments. Each micro-batch's targets name every passage of it once.
All inputs are finite; a program needn't handle non-finite values.
Results may differ from a plain program's by a relative error of at most 0.023.
Values may be sent and summed in bfloat16 or wider, within the bound.
A program may use at most 80 MiB of HBM per device.

v0:
```python
import functools
import math

import jax
import jax.numpy as jnp
from jax import lax
from jax.experimental import pallas as pl
from jax.experimental.pallas import tpu as pltpu
from jax.sharding import PartitionSpec as P

HEADS = 12


EPSILON = 1e-12
NEGATIVE = -1000000000.0
PRECISE = lax.Precision.HIGHEST


def passed_along(x, axis, by):
    size = lax.axis_size(axis)
    return lax.ppermute(x, axis, [(i, (i + by) % size) for i in range(size)])


def as_sent(x):
    return jax.tree.map(lambda a: a.astype(jnp.bfloat16) if a.dtype == jnp.float32 else a, x)


def layer_norm(values, norm_gain, norm_shift):
    center = values - jnp.mean(values, axis=-1, keepdims=True)
    factor = lax.rsqrt(jnp.mean(center * center, axis=-1, keepdims=True) + EPSILON)
    normed = center * factor
    return (normed * norm_gain + norm_shift, normed, factor)


def norm_back(gradient, normed, factor, norm_gain):
    scaled = gradient * norm_gain
    inner_term = (
        scaled
        - jnp.mean(scaled, axis=-1, keepdims=True)
        - normed * jnp.mean(scaled * normed, axis=-1, keepdims=True)
    )
    return inner_term * factor


def gelu_slope(values):
    normal_cdf = 0.5 * (1.0 + lax.erf(values * (1.0 / math.sqrt(2.0))))
    return normal_cdf + values * jnp.exp(-0.5 * values * values) * (1.0 / math.sqrt(2.0 * math.pi))


def scores_of(query_rows, key_rows, query_segment, key_segment, score_scale):
    raw_scores = jnp.einsum(
        "rqhd,rkhd->rhqk", query_rows, key_rows, preferred_element_type=jnp.float32
    )
    same_doc = (query_segment[:, :, None] == key_segment[:, None, :])[:, None]
    return jnp.where(same_doc, score_scale * raw_scores, NEGATIVE)


def contribute(
    query_rows,
    push_grad,
    delta_term,
    peak_term,
    query_segment,
    key_rows,
    value_rows,
    key_segment,
    score_scale,
):
    scores = scores_of(query_rows, key_rows, query_segment, key_segment, score_scale)
    weights = jnp.exp(scores - peak_term[..., None])
    pushed = jnp.einsum(
        "rqhd,rkhd->rhqk", push_grad, value_rows, preferred_element_type=jnp.float32
    )
    dscore = (weights * (pushed - delta_term[..., None]) * score_scale).astype(jnp.bfloat16)
    query_part = jnp.einsum("rhqk,rkhd->rqhd", dscore, key_rows, preferred_element_type=jnp.float32)
    key_part = jnp.einsum("rhqk,rqhd->rkhd", dscore, query_rows, preferred_element_type=jnp.float32)
    value_part = jnp.einsum(
        "rhqk,rqhd->rkhd",
        weights.astype(jnp.bfloat16),
        push_grad,
        preferred_element_type=jnp.float32,
    )
    return (query_part, key_part, value_part)


def ring_body(
    hidden_in,
    segment_ids,
    queries,
    targets,
    cotangent,
    query_weight,
    key_weight,
    value_weight,
    output_weight,
    query_bias,
    value_bias,
    output_bias,
    first_gain,
    first_shift,
    inner_weight,
    inner_bias,
    outer_weight,
    outer_bias,
    second_gain,
    second_shift,
):
    shards = (
        query_weight,
        key_weight,
        value_weight,
        output_weight,
        query_bias,
        value_bias,
        output_bias,
        first_gain,
        first_shift,
        inner_weight,
        inner_bias,
        outer_weight,
        outer_bias,
        second_gain,
        second_shift,
    )
    cycle_size = lax.axis_size("blk")
    cycle_place = lax.axis_index("blk")
    micro_count, row_count, block_tokens, model_width = hidden_in.shape
    segment_count = queries.shape[1] // row_count
    head_count = HEADS
    head_dim = model_width // head_count
    score_scale = 1.0 / math.sqrt(head_dim)
    token_count = row_count * block_tokens
    head_shape = (row_count, block_tokens, head_count, head_dim)
    grad_totals = tuple((jnp.zeros(shard_piece.shape, jnp.float32) for shard_piece in shards))
    local_sum = None
    gathered = None
    out_list, embed_list, loss_list, qgrad_list, hgrad_list = ([], [], [], [], [])
    for micro_index in range(micro_count):
        gathered = (
            lax.all_gather(shards[0], "dp", axis=0, tiled=True),
            lax.all_gather(shards[1], "dp", axis=0, tiled=True),
            lax.all_gather(shards[2], "dp", axis=0, tiled=True),
            lax.all_gather(shards[3], "dp", axis=0, tiled=True),
            lax.all_gather(shards[4], "dp", axis=0, tiled=True),
            lax.all_gather(shards[5], "dp", axis=0, tiled=True),
            lax.all_gather(shards[6], "dp", axis=0, tiled=True),
            lax.all_gather(shards[7], "dp", axis=0, tiled=True),
            lax.all_gather(shards[8], "dp", axis=0, tiled=True),
            lax.all_gather(shards[9], "dp", axis=0, tiled=True),
            lax.all_gather(shards[10], "dp", axis=0, tiled=True),
            lax.all_gather(shards[11], "dp", axis=0, tiled=True),
            lax.all_gather(shards[12], "dp", axis=0, tiled=True),
            lax.all_gather(shards[13], "dp", axis=0, tiled=True),
            lax.all_gather(shards[14], "dp", axis=0, tiled=True),
        )
        (
            wq_full,
            wk_full,
            wv_full,
            wo_full,
            bq_full,
            bv_full,
            bo_full,
            gain_one,
            shift_one,
            w_inner,
            b_inner,
            w_outer,
            b_outer,
            gain_two,
            shift_two,
        ) = gathered
        gain_one = gain_one.astype(jnp.float32)
        gain_two = gain_two.astype(jnp.float32)
        segment = segment_ids[micro_index]
        flat_rows = hidden_in[micro_index].reshape(token_count, model_width)
        query_rows = (
            (
                jnp.dot(flat_rows, wq_full, preferred_element_type=jnp.float32)
                + bq_full.astype(jnp.float32)
            )
            .astype(jnp.bfloat16)
            .reshape(head_shape)
        )
        key_rows = (
            jnp.dot(flat_rows, wk_full, preferred_element_type=jnp.float32)
            .astype(jnp.bfloat16)
            .reshape(head_shape)
        )
        value_rows = (
            (
                jnp.dot(flat_rows, wv_full, preferred_element_type=jnp.float32)
                + bv_full.astype(jnp.float32)
            )
            .astype(jnp.bfloat16)
            .reshape(head_shape)
        )

        def absorb(softmax_state, visit_keys, visit_values, visit_segment):
            running_peak, running_total, running_sum = softmax_state
            scores = scores_of(query_rows, visit_keys, segment, visit_segment, score_scale)
            new_peak = jnp.maximum(running_peak, jnp.max(scores, axis=-1))
            decay_factor = jnp.exp(running_peak - new_peak)
            weights = jnp.exp(scores - new_peak[..., None])
            running_total = running_total * decay_factor + jnp.sum(weights, axis=-1)
            update = jnp.einsum(
                "rhqk,rkhd->rqhd",
                weights.astype(jnp.bfloat16),
                visit_values,
                preferred_element_type=jnp.float32,
            )
            running_sum = running_sum * jnp.transpose(decay_factor, (0, 2, 1))[..., None] + update
            return (new_peak, running_total, running_sum)

        start_state = (
            jnp.full((row_count, head_count, block_tokens), -1e30, jnp.float32),
            jnp.zeros((row_count, head_count, block_tokens), jnp.float32),
            jnp.zeros(head_shape, jnp.float32),
        )
        first_state = absorb(start_state, key_rows, value_rows, segment)

        def forward_step(cycle_step, cycle_carry):
            visit_keys, visit_values, visit_segment, prior_segment, softmax_state = cycle_carry
            visit_keys, visit_values, visit_segment = passed_along(
                (visit_keys, visit_values, visit_segment), "blk", 1
            )
            prior_segment = jnp.where(cycle_step == 1, visit_segment[:, -1], prior_segment)
            return (
                visit_keys,
                visit_values,
                visit_segment,
                prior_segment,
                absorb(softmax_state, visit_keys, visit_values, visit_segment),
            )

        cycle_carry = lax.fori_loop(
            1, cycle_size, forward_step, (key_rows, value_rows, segment, segment[:, 0], first_state)
        )
        prior_segment = cycle_carry[3]
        row_peak, row_total, running_sum = cycle_carry[4]
        total_heads = jnp.transpose(row_total, (0, 2, 1))[..., None]
        context = running_sum / total_heads
        context_low = context.reshape(token_count, model_width).astype(jnp.bfloat16)
        attended = jnp.dot(
            context_low, wo_full, preferred_element_type=jnp.float32
        ) + bo_full.astype(jnp.float32)
        first_out, first_normed, first_factor = layer_norm(
            flat_rows.astype(jnp.float32) + attended, gain_one, shift_one.astype(jnp.float32)
        )
        first_low = first_out.astype(jnp.bfloat16)
        inner_pre = jnp.dot(
            first_low, w_inner, preferred_element_type=jnp.float32
        ) + b_inner.astype(jnp.float32)
        active = jax.nn.gelu(inner_pre, approximate=False).astype(jnp.bfloat16)
        outer_out = jnp.dot(active, w_outer, preferred_element_type=jnp.float32) + b_outer.astype(
            jnp.float32
        )
        output, second_normed, second_factor = layer_norm(
            first_out + outer_out, gain_two, shift_two.astype(jnp.float32)
        )
        output_low = output.astype(jnp.bfloat16)
        out_list.append(output_low.reshape(row_count, block_tokens, model_width))
        position = cycle_place * block_tokens + jnp.arange(block_tokens, dtype=jnp.int32)
        before = jnp.concatenate([prior_segment[:, None], segment[:, :-1]], axis=1)
        leading = (position[None, :] == 0) | (segment != before)
        numbers = jnp.arange(segment_count, dtype=jnp.int32)
        select = (leading[:, None, :] & (segment[:, None, :] == numbers[None, :, None])).astype(
            jnp.float32
        )
        cls_table = jnp.einsum(
            "rsi,rid->rsd",
            select.astype(jnp.bfloat16),
            output_low.reshape(row_count, block_tokens, model_width),
            preferred_element_type=jnp.float32,
        )
        own_table = lax.psum(cls_table.astype(jnp.bfloat16), "blk").reshape(
            row_count * segment_count, model_width
        )
        embed_list.append(own_table)
        everyone = lax.all_gather(own_table, "dp", axis=0, tiled=True)
        query_vectors = queries[micro_index]
        query_scores = jnp.dot(query_vectors, everyone.T, preferred_element_type=jnp.float32)
        score_peak = jnp.max(query_scores, axis=1, keepdims=True)
        log_total = score_peak[:, 0] + jnp.log(jnp.sum(jnp.exp(query_scores - score_peak), axis=1))
        target_hot = (
            jnp.arange(query_scores.shape[1], dtype=jnp.int32)[None, :]
            == targets[micro_index][:, None]
        ).astype(jnp.float32)
        loss_list.append(log_total - jnp.sum(query_scores * target_hot, axis=1))
        dscore_query = jnp.exp(query_scores - log_total[:, None]) - target_hot
        qgrad_list.append(jnp.dot(dscore_query, everyone.astype(jnp.float32), precision=PRECISE))
        embed_part = jnp.dot(dscore_query.T, query_vectors.astype(jnp.float32), precision=PRECISE)
        embed_grad = (
            lax.psum_scatter(embed_part.astype(jnp.bfloat16), "dp", scatter_dimension=0, tiled=True)
            .astype(jnp.float32)
            .reshape(row_count, segment_count, model_width)
        )
        cls_grad = jnp.einsum("rsi,rsd->rid", select, embed_grad, precision=PRECISE)
        dout = cotangent[micro_index].reshape(token_count, model_width).astype(
            jnp.float32
        ) + cls_grad.reshape(token_count, model_width)
        gain_two_grad = jnp.sum(dout * second_normed, axis=0)
        shift_two_grad = jnp.sum(dout, axis=0)
        dsecond = norm_back(dout, second_normed, second_factor, gain_two)
        douter = dsecond.astype(jnp.bfloat16)
        outer_bias_grad = jnp.sum(douter.astype(jnp.float32), axis=0)
        outer_weight_grad = jnp.einsum(
            "nf,nd->fd", active, douter, preferred_element_type=jnp.float32
        )
        dactive = jnp.einsum("nd,fd->nf", douter, w_outer, preferred_element_type=jnp.float32)
        dinner = (dactive * gelu_slope(inner_pre)).astype(jnp.bfloat16)
        inner_bias_grad = jnp.sum(dinner.astype(jnp.float32), axis=0)
        inner_weight_grad = jnp.einsum(
            "nd,nf->df", first_low, dinner, preferred_element_type=jnp.float32
        )
        dfirst = dsecond + jnp.einsum(
            "nf,df->nd", dinner, w_inner, preferred_element_type=jnp.float32
        )
        gain_one_grad = jnp.sum(dfirst * first_normed, axis=0)
        shift_one_grad = jnp.sum(dfirst, axis=0)
        dresidual = norm_back(dfirst, first_normed, first_factor, gain_one)
        dattended = dresidual.astype(jnp.bfloat16)
        output_bias_grad = jnp.sum(dattended.astype(jnp.float32), axis=0)
        output_weight_grad = jnp.einsum(
            "nd,ne->de", context_low, dattended, preferred_element_type=jnp.float32
        )
        dcontext = jnp.einsum(
            "ne,de->nd", dattended, wo_full, preferred_element_type=jnp.float32
        ).astype(jnp.bfloat16)
        dcontext_wide = dcontext.astype(jnp.float32).reshape(head_shape)
        push_grad = (dcontext_wide / total_heads).astype(jnp.bfloat16)
        delta_term = jnp.transpose(
            jnp.sum(dcontext_wide * context, axis=-1) / total_heads[..., 0], (0, 2, 1)
        )
        own_query, own_key, own_value = contribute(
            query_rows,
            push_grad,
            delta_term,
            row_peak,
            segment,
            key_rows,
            value_rows,
            segment,
            score_scale,
        )

        def key_step(cycle_step, cycle_carry):
            visit_keys, visit_values, visit_segment, query_sum, key_sum, value_sum = cycle_carry
            visit_keys, visit_values, visit_segment = passed_along(
                (visit_keys, visit_values, visit_segment), "blk", 1
            )
            key_sum, value_sum = (
                passed_along(key_sum.astype(jnp.bfloat16), "blk", 1).astype(key_sum.dtype),
                passed_along(value_sum.astype(jnp.bfloat16), "blk", 1).astype(value_sum.dtype),
            )
            query_part, key_part, value_part = contribute(
                query_rows,
                push_grad,
                delta_term,
                row_peak,
                segment,
                visit_keys,
                visit_values,
                visit_segment,
                score_scale,
            )
            return (
                visit_keys,
                visit_values,
                visit_segment,
                query_sum + query_part,
                key_sum + key_part,
                value_sum + value_part,
            )

        back_carry = lax.fori_loop(
            1, cycle_size, key_step, (key_rows, value_rows, segment, own_query, own_key, own_value)
        )
        query_sum = back_carry[3]
        key_sum, value_sum = (
            passed_along(back_carry[4].astype(jnp.bfloat16), "blk", 1).astype(jnp.float32),
            passed_along(back_carry[5].astype(jnp.bfloat16), "blk", 1).astype(jnp.float32),
        )
        dquery = query_sum.astype(jnp.bfloat16).reshape(token_count, model_width)
        dkey = key_sum.astype(jnp.bfloat16).reshape(token_count, model_width)
        dvalue = value_sum.astype(jnp.bfloat16).reshape(token_count, model_width)
        dhidden = dresidual + jnp.einsum(
            "ne,de->nd", dquery, wq_full, preferred_element_type=jnp.float32
        )
        dhidden = dhidden + jnp.einsum(
            "ne,de->nd", dkey, wk_full, preferred_element_type=jnp.float32
        )
        dhidden = dhidden + jnp.einsum(
            "ne,de->nd", dvalue, wv_full, preferred_element_type=jnp.float32
        )
        hgrad_list.append(
            dhidden.astype(jnp.bfloat16).reshape(row_count, block_tokens, model_width)
        )
        local_grads = (
            jnp.einsum("nd,ne->de", flat_rows, dquery, preferred_element_type=jnp.float32),
            jnp.einsum("nd,ne->de", flat_rows, dkey, preferred_element_type=jnp.float32),
            jnp.einsum("nd,ne->de", flat_rows, dvalue, preferred_element_type=jnp.float32),
            output_weight_grad,
            jnp.sum(dquery.astype(jnp.float32), axis=0),
            jnp.sum(dvalue.astype(jnp.float32), axis=0),
            output_bias_grad,
            gain_one_grad,
            shift_one_grad,
            inner_weight_grad,
            inner_bias_grad,
            outer_weight_grad,
            outer_bias_grad,
            gain_two_grad,
            shift_two_grad,
        )
        local_sum = local_grads
        reduced = jax.tree.map(
            lambda part: part.astype(jnp.float32),
            lax.psum_scatter(as_sent(local_sum), "dp", scatter_dimension=0, tiled=True),
        )
        reduced = jax.tree.map(
            lambda part: part.astype(jnp.float32), lax.psum(as_sent(reduced), "blk")
        )
        grad_totals = tuple(
            (total_piece + new_piece for total_piece, new_piece in zip(grad_totals, reduced))
        )
        local_sum = None
    return (
        jnp.stack(out_list),
        jnp.stack(embed_list),
        jnp.stack(loss_list),
        jnp.stack(qgrad_list),
        jnp.stack(hgrad_list),
        grad_totals[0],
        grad_totals[1],
        grad_totals[2],
        grad_totals[3],
        grad_totals[4],
        grad_totals[5],
        grad_totals[6],
        grad_totals[7],
        grad_totals[8],
        grad_totals[9],
        grad_totals[10],
        grad_totals[11],
        grad_totals[12],
        grad_totals[13],
        grad_totals[14],
    )


MESH = pl.DeviceIdType.MESH
VMEM_LIMIT = 60 * 1024 * 1024
SIDE = {"c": 1, "x": 2, "y": 4}


def place():
    dp, blk = lax.axis_index("dp"), lax.axis_index("blk")
    bits = {"c": lax.rem(dp, 2), "x": lax.rem(dp // 2, 2), "y": dp // 4}
    return dp, blk, bits


def across(dp, blk, bits, *axes):
    other = dp
    for axis in axes:
        other = other + SIDE[axis] * (1 - 2 * bits[axis])
    return (other, blk)


def greet(peers):
    barrier = pltpu.get_barrier_semaphore()
    for peer in peers:
        pl.semaphore_signal(barrier, inc=1, device_id=peer, device_id_type=MESH)
    pl.semaphore_wait(barrier, len(peers))


def remote(source, target, send_sem, recv_sem, peer):
    return pltpu.make_async_remote_copy(
        src_ref=source,
        dst_ref=target,
        send_sem=send_sem,
        recv_sem=recv_sem,
        device_id=peer,
        device_id_type=MESH,
    )


def comm_params(collective):
    return pltpu.CompilerParams(
        collective_id=collective, has_side_effects=True, vmem_limit_bytes=VMEM_LIMIT
    )


ANY = pl.BlockSpec(memory_space=pl.ANY)
IN_VMEM = pl.BlockSpec(memory_space=pltpu.VMEM)


SLABS = 2


def forward_kernel(items, ring_size, depth, sources, places, *refs):
    shards, seg_shard, hidden = refs[:sources], refs[sources], refs[sources + 1]
    outs = refs[sources + 2 :]
    fulls = outs[:places]
    seg_full, hidden_row, qkv, context, stats, context_t = outs[places : places + 6]
    (
        hidden_full,
        low,
        seg_line,
        mask,
        turned,
        keys,
        send_sem,
        recv_sem,
        seg_send,
        seg_recv,
        line_send,
        line_recv,
        head_send,
        head_recv,
        local_sem,
    ) = outs[places + 6 :]
    w_window, pack_full = fulls[0], fulls[1]
    dp, blk, bits = place()
    sibling = across(dp, blk, bits, "c")
    ring = [(dp, lax.rem(blk + step, ring_size)) for step in range(1, ring_size)]
    greet([sibling, across(dp, blk, bits, "x"), across(dp, blk, bits, "y")] + ring)
    seg_rows = seg_shard.shape[0]
    micro, tokens, width = hidden.shape
    spread = ring_size // micro
    row_at, group_at = blk // spread, lax.rem(blk, spread)
    group, length = context.shape
    heads = group // depth
    score_scale = 1.0 / math.sqrt(depth)
    waiting = []
    mine = pl.ds(pl.multiple_of(blk * tokens, tokens), tokens)

    slab = tokens // SLABS

    def line_view(m, side, distance, part):
        owner = blk + (1 - 2 * side) * distance
        first = owner * tokens + part * slab
        return hidden_full.at[m, pl.ds(pl.multiple_of(first, slab), slab)]

    def line_copy(m, side, distance, part):
        view = line_view(m, side, distance, part)
        return remote(
            hidden.at[m, pl.ds(part * slab, slab)] if distance == 0 else view,
            view,
            line_send.at[m, side, distance, part],
            line_recv.at[m, side, distance + 1, part],
            (dp, blk - 1 + 2 * side),
        )

    def arrival(m, side, distance, part):
        view = line_view(m, side, distance, part)
        return remote(
            view,
            view,
            line_send.at[m, side, distance, part],
            line_recv.at[m, side, distance, part],
            (dp, blk - 1 + 2 * side),
        )

    def passes_on(m, side):
        return blk > m * spread if side == 0 else blk < m * spread + spread - 1

    def comes(m, side, distance):
        if side == 0:
            return (blk >= m * spread) & (blk + distance < ring_size)
        return (blk < m * spread + spread) & (blk >= distance)

    def line_step(distance, part):
        for m in range(micro):
            for side in range(2):

                @pl.when(comes(m, side, distance))
                def _():
                    arrival(m, side, distance, part).wait_recv()

                if distance < ring_size - 1:

                    @pl.when(comes(m, side, distance) & passes_on(m, side))
                    def _():
                        line_copy(m, side, distance, part).start()

    for part in range(SLABS):
        for m in range(micro):
            for side in range(2):

                @pl.when(passes_on(m, side))
                def _():
                    line_copy(m, side, 0, part).start()

    def own_part(item):
        spec = items[item]
        column = spec["from_column"]
        if column is None:
            column = pl.multiple_of(group_at * group, group)
        return shards[spec["source"]].at[
            pl.ds(spec["row"], spec["rows"]), pl.ds(column, spec["columns"])
        ]

    def block(item, owner):
        spec = items[item]
        first = owner * spec["stride"] + spec["row"]
        return fulls[spec["target"]].at[
            pl.ds(first, spec["rows"]), pl.ds(spec["to_column"], spec["columns"])
        ]

    inbound = {}

    def start_item(item):
        first, second = items[item]["route"]
        for slot, peer in enumerate(
            (across(dp, blk, bits, first), across(dp, blk, bits, second), sibling)
        ):
            copy = remote(
                own_part(item),
                block(item, dp),
                send_sem.at[item, slot],
                recv_sem.at[item, slot],
                peer,
            )
            copy.start()
            inbound[item, slot] = copy
        copy = pltpu.make_async_copy(own_part(item), block(item, dp), local_sem.at[item])
        copy.start()
        inbound[item, "own"] = copy

    def pass_on(item, held, slot, peer):
        copy = remote(held, held, send_sem.at[item, slot], recv_sem.at[item, slot], peer)
        copy.start()
        inbound[item, slot] = copy

    def relay_first(item):
        first, second = items[item]["route"]
        inbound[item, 0].wait_recv()
        held = block(item, across(dp, blk, bits, first)[0])
        pass_on(item, held, 3, across(dp, blk, bits, second))
        pass_on(item, held, 4, sibling)
        inbound[item, 1].wait_recv()
        pass_on(item, block(item, across(dp, blk, bits, second)[0]), 5, sibling)

    def relay_third(item):
        first, second = items[item]["route"]
        inbound[item, 3].wait_recv()
        pass_on(item, block(item, across(dp, blk, bits, first, second)[0]), 6, sibling)

    def all_here(item):
        for slot in (2, 4, 5, 6):
            inbound[item, slot].wait_recv()
        inbound[item, "own"].wait()

    early = [i for i, spec in enumerate(items) if spec["target"] < 2]
    late = [i for i, spec in enumerate(items) if spec["target"] >= 2]
    tick_of = [0]

    def tick(times=1):
        for _ in range(times):
            now = tick_of[0]
            tick_of[0] += 1
            if 0 <= now - 2 * LAG < len(late):
                relay_third(late[now - 2 * LAG])
            if 0 <= now - LAG < len(late):
                relay_first(late[now - LAG])
            if now < len(late):
                start_item(late[now])

    for item in early:
        start_item(item)
    for step, peer in enumerate(ring):
        copy = remote(
            seg_shard,
            seg_full.at[pl.ds(blk * seg_rows, seg_rows)],
            seg_send.at[step],
            seg_recv.at[step],
            peer,
        )
        copy.start()
        waiting.append(copy)
    seg_full[pl.ds(blk * seg_rows, seg_rows)] = seg_shard[...]

    for item in early:
        relay_first(item)
    tick()
    line_step(1, 0)
    tick()
    for part in range(1, SLABS):
        line_step(1, part)
    for item in early:
        relay_third(item)
    tick()
    for copy in waiting:
        copy.wait()
    for member in range(ring_size):
        seg_line[:, member * tokens : (member + 1) * tokens] = seg_full[
            pl.ds(member * seg_rows + row_at, 1)
        ].astype(jnp.float32)
    seg_col = columns_of(seg_line[...])
    for item in early:
        all_here(item)
    pack_turned = pack_full[...].astype(jnp.float32).T
    piece = width // (pack_full.shape[0] // 16)
    lane = lax.broadcasted_iota(jnp.int32, (piece, pack_full.shape[0]), 1)

    def bias_column(vector):
        pieces = []
        for part in range(group // piece):
            at = (group_at * (group // piece) + part) * 16 + vector
            pieces.append(
                jnp.sum(
                    jnp.where(lane == at, pack_turned[:piece], 0.0), axis=1, keepdims=True
                )
            )
        return jnp.concatenate(pieces, axis=0)

    biases = (bias_column(0), None, bias_column(1))
    for part in range(3):
        rows = slice(part * group, (part + 1) * group)
        turned[rows, :] = w_window[:, rows].T

    def project(at, source):
        span = pl.ds(pl.multiple_of(at * tokens, tokens), tokens)
        values = source[...]
        hidden_row[span, :] = values
        for part in range(3):
            rows = slice(part * group, (part + 1) * group)
            result = contract(turned[rows, :], values, 1, 1)
            if biases[part] is not None:
                result = result + biases[part]
            qkv[rows, span] = result.astype(jnp.bfloat16)

    def project_at(distance):
        for side in range(2):
            at = blk + (1 - 2 * side) * distance

            @pl.when((at >= 0) & (at < ring_size))
            def _():
                view = hidden_full.at[row_at, pl.ds(pl.multiple_of(at * tokens, tokens), tokens)]
                project(at, view)

    if ring_size > 2:
        line_step(2, 0)
    project(blk, hidden.at[row_at])
    tick()
    project_at(1)
    for distance in range(2, ring_size):
        for part in range(SLABS):
            if distance > 2 or part > 0:
                line_step(distance, part)
                tick()
        project_at(distance)

    copies = []

    def head_rows(part, head):
        first = part * group + head * depth
        return slice(first, first + depth)

    for head in range(heads):
        keys[head] = qkv[head_rows(1, head), :].T

    def attend(at):
        span = pl.ds(pl.multiple_of(at * tokens, tokens), tokens)
        mask[...] = jnp.where(seg_col == seg_line[:, span], 0.0, NEGATIVE)
        for head in range(heads):
            rows = head_rows(0, head)
            queries = (qkv[rows, span].astype(jnp.float32) * score_scale).astype(jnp.bfloat16)
            scores = contract(keys[head], queries, 1, 0) + mask[...]
            peak = jnp.max(scores, axis=0, keepdims=True)
            weights = jnp.exp(scores - peak)
            total = jnp.sum(weights, axis=0, keepdims=True)
            ctx = contract(qkv[head_rows(2, head), :], weights.astype(jnp.bfloat16), 1, 0) / total
            context[rows, span] = ctx
            low[rows, span] = ctx.astype(jnp.bfloat16)
            stats[2 * head : 2 * head + 1, span] = peak
            stats[2 * head + 1 : 2 * head + 2, span] = total

    end = (ring_size - 1) * (1 - row_at)
    order = (end, end + 2 * row_at - 1, blk + 1 - 2 * lax.rem(blk, 2), blk)
    target = context_t.at[row_at, pl.ds(group_at * group, group)]
    for index, at in enumerate(order):
        attend(at)
        span = pl.ds(pl.multiple_of(at * tokens, tokens), tokens)
        if index < ring_size - 1:
            step = lax.rem(at - blk + ring_size, ring_size)
            copy = remote(low.at[:, span], target, head_send.at[index], head_recv.at[step], (dp, at))
            copy.start()
            copies.append(copy)
        else:
            target[...] = low[:, span]
        tick(2)
    tick(len(late) + 2 * LAG - tick_of[0])
    for item in late:
        all_here(item)
    for item in early + late:
        for slot in range(7):
            inbound[item, slot].wait_send()
    for copy in copies:
        copy.wait_send()
    for step, peer in enumerate(ring):
        remote(target, target, head_send.at[0], head_recv.at[step + 1], peer).wait_recv()
    for m in range(micro):
        for side in range(2):
            for distance in range(ring_size - 1):
                ready = passes_on(m, side)
                if distance:
                    ready = ready & comes(m, side, distance)

                @pl.when(ready)
                def _():
                    for part in range(SLABS):
                        line_copy(m, side, distance, part).wait_send()


def columns_of(row):
    return jnp.broadcast_to(row, (128, row.shape[1])).T[:, :1]


def forward(shards, items, targets, segments, hidden, ring_size, depth):
    micro, tokens, width = hidden.shape
    count = len(shards)
    length = ring_size * tokens
    group = width * micro // ring_size
    heads = group // depth
    shape = jax.ShapeDtypeStruct
    return pl.pallas_call(
        functools.partial(forward_kernel, items, ring_size, depth, count, len(targets)),
        out_shape=tuple(targets)
        + (
            shape((ring_size * segments.shape[0], tokens), jnp.int32),
            shape((length, width), jnp.bfloat16),
            shape((3 * group, length), jnp.bfloat16),
            shape((group, length), jnp.float32),
            shape((2 * heads, length), jnp.float32),
            shape((micro, width, tokens), jnp.bfloat16),
        ),
        in_specs=[IN_VMEM] * (count + 2),
        out_specs=(IN_VMEM, IN_VMEM) + (ANY,) * (len(targets) - 2) + (IN_VMEM,) * 6,
        scratch_shapes=[
            pltpu.VMEM((micro, length, width), jnp.bfloat16),
            pltpu.VMEM((group, length), jnp.bfloat16),
            pltpu.VMEM((1, length), jnp.float32),
            pltpu.VMEM((length, tokens), jnp.float32),
            pltpu.VMEM((3 * group, width), jnp.bfloat16),
            pltpu.VMEM((heads, length, depth), jnp.bfloat16),
            pltpu.SemaphoreType.DMA((len(items), 7)),
            pltpu.SemaphoreType.DMA((len(items), 7)),
            pltpu.SemaphoreType.DMA((ring_size,)),
            pltpu.SemaphoreType.DMA((ring_size,)),
            pltpu.SemaphoreType.DMA((micro, 2, ring_size, SLABS)),
            pltpu.SemaphoreType.DMA((micro, 2, ring_size, SLABS)),
            pltpu.SemaphoreType.DMA((ring_size,)),
            pltpu.SemaphoreType.DMA((ring_size,)),
            pltpu.SemaphoreType.DMA((len(items),)),
        ],
        compiler_params=comm_params(1),
    )(*shards, segments, hidden)


def contract(left, right, left_dim, right_dim):
    return lax.dot_general(
        left, right, (((left_dim,), (right_dim,)), ((), ())), preferred_element_type=jnp.float32
    )


LAG, AHEAD = 2, 3


def added(left, right):
    return (left.astype(jnp.float32) + right.astype(jnp.float32)).astype(jnp.bfloat16)


def backward_kernel(items, ring_size, depth, *refs):
    (
        dcontext_part,
        seg_row,
        pack_part,
        qkv_out,
        context_out,
        stats,
        w_window_out,
        hidden_row_out,
        dresidual_out,
        outer_grad,
        inner_grad,
        output_grad,
    ) = refs[:12]
    dhidden, d_outer, d_inner, d_output, d_window, d_pack = refs[12:18]
    (
        qkv,
        context,
        w_window,
        hidden_row,
        dresidual,
        dcontext,
        dwindow,
        parts,
        passed,
        arrived,
        window_grad,
        pack_sum,
        pack_low,
        own,
        from_core,
        from_first,
        from_second,
        ring_one,
        ring_two,
        load_sem,
        head_send,
        head_recv,
        hop_send,
        hop_recv,
        send_sem,
        recv_sem,
        local_sem,
    ) = refs[18:]
    grads = (outer_grad, inner_grad, output_grad, window_grad, pack_low)
    outs = (d_outer, d_inner, d_output, d_window, d_pack)
    count = len(items)
    dp, blk, bits = place()
    sibling = across(dp, blk, bits, "c")
    is_end = (blk == 0) | (blk == ring_size - 1)
    is_middle = jnp.logical_not(is_end)
    partner = (dp, blk + 1 - 2 * lax.rem(blk, 2))
    facing = (dp, ring_size - 1 - blk)
    ring = [(dp, lax.rem(blk + step, ring_size)) for step in range(1, ring_size)]
    greet([sibling, across(dp, blk, bits, "x"), across(dp, blk, bits, "y")] + ring)

    micro, width, tokens = dcontext_part.shape
    spread = ring_size // micro
    row_at, group_at = blk // spread, lax.rem(blk, spread)
    group, length = context.shape
    heads = group // depth
    score_scale = 1.0 / math.sqrt(depth)
    mine = pl.ds(pl.multiple_of(blk * tokens, tokens), tokens)

    loads = []
    for index, (source, target) in enumerate(
        (
            (qkv_out, qkv),
            (context_out, context),
            (w_window_out, w_window),
            (hidden_row_out, hidden_row),
            (dresidual_out, dresidual),
        )
    ):
        copy = pltpu.make_async_copy(source, target, load_sem.at[index])
        copy.start()
        loads.append(copy)

    head_copies = []
    def send_head(head):
        for step in range(1, ring_size):
            owner = lax.rem(blk + step, ring_size)
            first = lax.rem(owner, spread) * group + head * depth
            copy = remote(
                dcontext_part.at[owner // spread, pl.ds(first, depth)],
                dcontext.at[pl.ds(head * depth, depth), mine],
                head_send.at[head, step],
                head_recv.at[head, step],
                (dp, owner),
            )
            copy.start()
            head_copies.append(copy)
    send_head(0)
    send_head(1)
    dcontext[:, mine] = dcontext_part[row_at, pl.ds(group_at * group, group)]

    def owner_of(core, axes, first_bit, second_bit):
        return core + SIDE[axes[0]] * first_bit + SIDE[axes[1]] * second_bit

    def block(item, which):
        spec = items[item]
        return grads[spec["source"]].at[
            pl.ds(which * spec["stride"] + spec["row"], spec["rows"]),
            pl.ds(spec["column"], spec["columns"]),
        ]

    def cut(buffer, item, *index):
        spec = items[item]
        return buffer.at[(item,) + index + (pl.ds(0, spec["rows"]), pl.ds(0, spec["columns"]))]

    def wide_cut(buffer, item, *index):
        spec = items[item]
        columns = spec["columns"] * spec["widened"]
        return buffer.at[(item,) + index + (pl.ds(0, spec["rows"]), pl.ds(0, columns))]

    def result(item):
        spec = items[item]
        many = spec["widened"]
        return outs[spec["source"]].at[
            pl.ds(spec["row"], spec["rows"]),
            pl.ds(spec["column"] * many, spec["columns"] * many),
        ]

    def copier(source, target, item, slot, peer):
        return remote(source, target, send_sem.at[item, slot], recv_sem.at[item, slot], peer)

    flying = {}

    def go(source, target, item, slot, peer):
        copy = copier(source, target, item, slot, peer)
        copy.start()
        flying[item, slot] = copy

    def start_core(item):
        axes = items[item]["route"]
        for f in range(2):
            for s in range(2):
                slot = 2 * f + s
                go(
                    block(item, owner_of(1 - bits["c"], axes, f, s)),
                    cut(from_core, item, f, s),
                    item,
                    slot,
                    sibling,
                )
                copy = pltpu.make_async_copy(
                    block(item, owner_of(bits["c"], axes, f, s)),
                    cut(own, item, f, s),
                    local_sem.at[item, slot],
                )
                copy.start()
                flying[item, "own", slot] = copy

    def after_core(item):
        axes = items[item]["route"]
        kept = bits[axes[0]]
        for slot in range(4):
            flying[item, slot].wait_recv()
            flying[item, "own", slot].wait()
        for stays, f in ((False, 1 - kept), (True, kept)):
            for s in range(2):
                part = cut(own, item, f, s)
                part[...] = added(part[...], cut(from_core, item, f, s)[...])
                if not stays:
                    peer = across(dp, blk, bits, axes[0])
                    go(part, cut(from_first, item, s), item, 4 + s, peer)

    def after_first(item):
        axes = items[item]["route"]
        f, kept = bits[axes[0]], bits[axes[1]]
        for s in range(2):
            flying[item, 4 + s].wait_recv()
        part = cut(own, item, f, 1 - kept)
        part[...] = added(part[...], cut(from_first, item, 1 - kept)[...])
        go(part, cut(from_second, item), item, 6, across(dp, blk, bits, axes[1]))
        part = cut(own, item, f, kept)
        part[...] = added(part[...], cut(from_first, item, kept)[...])

    def after_second(item):
        spec = items[item]
        axes = spec["route"]
        f, s = bits[axes[0]], bits[axes[1]]
        flying[item, 6].wait_recv()
        total = added(cut(own, item, f, s)[...], cut(from_second, item)[...])
        if spec["widened"] > 1:
            wide_cut(ring_one, item, 0)[...] = jnp.zeros(
                (spec["rows"], spec["columns"] * spec["widened"]), jnp.bfloat16
            )
            at = pl.multiple_of(group_at * spec["columns"], 128)
            ring_one[item, 0, pl.ds(0, spec["rows"]), pl.ds(at, spec["columns"])] = total
        else:
            wide_cut(ring_one, item, 0)[...] = total
        flying[item, 7] = copier(
            wide_cut(ring_one, item, 0), wide_cut(ring_one, item, 1), item, 7, partner
        )
        flying[item, 8] = copier(
            wide_cut(ring_two, item, 0), wide_cut(ring_two, item, 1), item, 8, facing
        )
        flying[item, 9] = copier(result(item), result(item), item, 9, partner)

        @pl.when(is_end)
        def _():
            flying[item, 7].start()

    def at_middle(item):
        @pl.when(is_middle)
        def _():
            flying[item, 7].wait_recv()
            part = wide_cut(ring_two, item, 0)
            part[...] = added(wide_cut(ring_one, item, 0)[...], wide_cut(ring_one, item, 1)[...])
            flying[item, 8].start()

    def across_middle(item):
        @pl.when(is_middle)
        def _():
            flying[item, 8].wait_recv()
            result(item)[...] = added(
                wide_cut(ring_two, item, 0)[...], wide_cut(ring_two, item, 1)[...]
            )
            flying[item, 9].start()

    def at_end(item):
        @pl.when(is_end)
        def _():
            flying[item, 9].wait_recv()

    stages = (after_core, after_first, after_second, at_middle, across_middle, at_end)
    tick_of = [0]

    def tick(times=1):
        for _ in range(times):
            now = tick_of[0]
            tick_of[0] += 1
            for stage in reversed(range(len(stages))):
                item = now - LAG * stage
                if 0 <= item < count:
                    stages[stage](item)
            if now + AHEAD < len(early):
                start_core(early[now + AHEAD])

    early = [i for i, spec in enumerate(items) if spec["source"] < 3]
    late = [i for i, spec in enumerate(items) if spec["source"] >= 3]
    for item in early[:AHEAD]:
        start_core(item)

    seg_line = seg_row[...].astype(jnp.float32)
    seg_col = columns_of(seg_line)

    def one_head(head):
        def rows(part):
            first = part * group + head * depth
            return slice(first, first + depth)

        for step in range(ring_size - 1):
            head_copies[head * (ring_size - 1) + step].wait_recv()
        keys, values = qkv[rows(1), :].T, qkv[rows(2), :].T
        keys_t = qkv[rows(1), :]
        dkey_sum = jnp.zeros((depth, length), jnp.float32)
        dvalue_sum = jnp.zeros((depth, length), jnp.float32)
        for start in range(0, length, tokens):
            span = slice(start, start + tokens)
            peak = stats[2 * head : 2 * head + 1, span]
            total = stats[2 * head + 1 : 2 * head + 2, span]
            dctx = dcontext[rows(0), span].astype(jnp.float32)
            push = (dctx / total).astype(jnp.bfloat16)
            delta = jnp.sum(dctx * context[rows(0), span], axis=0, keepdims=True) / total
            queries_t = qkv[rows(0), span]
            raw = contract(keys, queries_t, 1, 0)
            same = seg_col == seg_line[:, span]
            weights = jnp.exp(jnp.where(same, raw * score_scale, NEGATIVE) - peak)
            pushed = contract(values, push, 1, 0)
            dscore = (weights * (pushed - delta) * score_scale).astype(jnp.bfloat16)
            dwindow[rows(0), span] = contract(keys_t, dscore, 1, 0).astype(jnp.bfloat16)
            dkey_sum = dkey_sum + contract(queries_t, dscore, 1, 1)
            dvalue_sum = dvalue_sum + contract(push, weights.astype(jnp.bfloat16), 1, 1)
        dwindow[rows(1), :] = dkey_sum.astype(jnp.bfloat16)
        dwindow[rows(2), :] = dvalue_sum.astype(jnp.bfloat16)

    loads[0].wait()
    loads[1].wait()
    for head in range(heads):
        if head + 2 < heads:
            send_head(head + 2)
        one_head(head)
        tick()
    loads[2].wait()
    loads[3].wait()
    loads[4].wait()

    low = [m * spread for m in range(micro)]
    high = [m * spread + spread - 1 for m in range(micro)]

    def owns(m):
        return (blk >= low[m]) & (blk <= high[m])

    def receives(m, side):
        return blk + 1 <= high[m] if side == 0 else blk - 1 >= low[m]

    def has_target(side, distance):
        return blk >= distance if side == 0 else blk + distance < ring_size

    def hop(source, m, side, distance):
        return remote(
            source,
            arrived.at[m, side, distance - 1],
            hop_send.at[m, side, distance],
            hop_recv.at[m, side, distance - 1],
            (dp, blk - 1 + 2 * side),
        )

    def arrival(m, side, distance):
        view = arrived.at[m, side, distance]
        return remote(
            view,
            view,
            hop_send.at[m, side, distance],
            hop_recv.at[m, side, distance],
            (dp, blk - 1 + 2 * side),
        )

    def send_fresh(distance):
        for m in range(micro):
            for side in range(2):
                target = blk - distance * (1 - 2 * side)
                goes = has_target(side, distance) & owns(m)

                @pl.when(goes & jnp.logical_not(receives(m, side)))
                def _():
                    hop(parts.at[target], m, side, distance).start()

    def send_on(distance):
        for m in range(micro):
            for side in range(2):
                target = blk - distance * (1 - 2 * side)
                goes = has_target(side, distance) & receives(m, side)

                @pl.when(goes & owns(m))
                def _():
                    arrival(m, side, distance).wait_recv()
                    passed[side, distance - 1] = added(parts[target], arrived[m, side, distance])
                    hop(passed.at[side, distance - 1], m, side, distance).start()

                @pl.when(goes & jnp.logical_not(owns(m)))
                def _():
                    arrival(m, side, distance).wait_recv()
                    hop(arrived.at[m, side, distance], m, side, distance).start()

    def finish_hidden(_):
        for m in range(micro):
            for side in range(2):
                inside = blk < ring_size - 1 if side == 0 else blk > 0
                here = receives(m, side) & inside

                @pl.when(here & owns(m))
                def _():
                    arrival(m, side, 0).wait_recv()
                    dhidden[m] = (
                        dresidual[m]
                        + parts[blk].astype(jnp.float32)
                        + arrived[m, side, 0].astype(jnp.float32)
                    ).astype(jnp.bfloat16)

                @pl.when(here & jnp.logical_not(owns(m)))
                def _():
                    arrival(m, side, 0).wait_recv()
                    dhidden[m] = (
                        dresidual[m] + arrived[m, side, 0].astype(jnp.float32)
                    ).astype(jnp.bfloat16)

    end = (ring_size - 1) * (1 - row_at)
    inward = 2 * row_at - 1
    order = (end, end + inward, blk + 1 - 2 * lax.rem(blk, 2), blk)

    def make_part(target):
        at = pl.ds(pl.multiple_of(target * tokens, tokens), tokens)
        parts[target] = contract(dwindow[:, at].T, w_window[...], 1, 1).astype(jnp.bfloat16)

    ones = jnp.ones((8, length), jnp.bfloat16)
    line = lax.broadcasted_iota(jnp.int32, (8, 128), 0)
    lane = lax.broadcasted_iota(jnp.int32, (8, 128), 1)
    piece = width // (pack_part.shape[0] // 16)
    pack_sum[...] = pack_part[...]

    def make_grad(part):
        rows = slice(part * group, (part + 1) * group)
        window_grad[:, rows] = contract(hidden_row[...].T, dwindow[rows, :], 1, 1).astype(
            jnp.bfloat16
        )
        if part != 1:
            sums = contract(ones, dwindow[rows, :], 1, 1)
            sums = jnp.concatenate((sums, jnp.zeros((8, 128), jnp.float32)), axis=1)
            for step in range(group // piece):
                first = pl.multiple_of((group_at * (group // piece) + step) * 16, 16)
                pack_sum[pl.ds(first, 8), 0:128] += jnp.where(
                    (line == part // 2) & (lane < piece),
                    sums[:, step * piece : step * piece + 128],
                    0.0,
                )
        start_core(late[part])

    for index, target in enumerate(order):
        make_part(target)
        if index < ring_size - 1:
            send_fresh(ring_size - 1 - index)
            make_grad(index)
            tick()
    pack_low[...] = pack_sum[...].astype(jnp.bfloat16)
    start_core(late[3])
    for distance in reversed(range(1, ring_size - 1)):
        send_on(distance)
        tick(2)
    finish_hidden(None)
    tick(count + LAG * (len(stages) - 1) - tick_of[0])

    for copy in head_copies:
        copy.wait_send()
    for item in range(count):
        for slot in range(7):
            flying[item, slot].wait_send()
    for distance in range(1, ring_size):
        for m in range(micro):
            for side in range(2):

                @pl.when(has_target(side, distance) & (receives(m, side) | owns(m)))
                def _():
                    hop(parts.at[0], m, side, distance).wait_send()

    @pl.when(is_end)
    def _():
        for item in range(count):
            flying[item, 7].wait_send()

    @pl.when(is_middle)
    def _():
        for item in range(count):
            flying[item, 8].wait_send()
            flying[item, 9].wait_send()


def backward(
    dcontext_part,
    seg_row,
    pack_part,
    saved,
    w_window,
    hidden_row,
    dresidual,
    grads,
    items,
    ring_size,
    dp_size,
    depth,
    collective,
):
    qkv, context, stats = saved
    micro, width, tokens = dcontext_part.shape
    group, length = context.shape
    heads = group // depth
    spread = ring_size // micro
    count = len(items)
    rows = max(item["rows"] for item in items)
    columns = max(item["columns"] * item["widened"] for item in items)
    piece = (rows, columns)
    narrow = jnp.bfloat16
    shape = jax.ShapeDtypeStruct
    outs = [shape((grad.shape[0] // dp_size, grad.shape[1]), narrow) for grad in grads]
    outs.append(shape((width // dp_size, 3 * width), narrow))
    outs.append(shape((pack_part.shape[0] // dp_size, pack_part.shape[1]), narrow))
    scratch = [
        pltpu.VMEM(qkv.shape, narrow),
        pltpu.VMEM(context.shape, jnp.float32),
        pltpu.VMEM(w_window.shape, narrow),
        pltpu.VMEM(hidden_row.shape, narrow),
        pltpu.VMEM(dresidual.shape, jnp.float32),
        pltpu.VMEM((group, length), narrow),
        pltpu.VMEM(qkv.shape, narrow),
        pltpu.VMEM((ring_size, tokens, width), narrow),
        pltpu.VMEM((2, ring_size - 2, tokens, width), narrow),
        pltpu.VMEM((micro, 2, ring_size - 1, tokens, width), narrow),
        pltpu.VMEM((width, 3 * group), narrow),
        pltpu.VMEM(pack_part.shape, jnp.float32),
        pltpu.VMEM(pack_part.shape, narrow),
    ]
    scratch += [
        pltpu.VMEM((count,) + lead + piece, narrow)
        for lead in ((2, 2), (2, 2), (2,), (), (2,), (2,))
    ]
    scratch += [
        pltpu.SemaphoreType.DMA((5,)),
        pltpu.SemaphoreType.DMA((heads, ring_size)),
        pltpu.SemaphoreType.DMA((heads, ring_size)),
        pltpu.SemaphoreType.DMA((micro, 2, ring_size)),
        pltpu.SemaphoreType.DMA((micro, 2, ring_size)),
        pltpu.SemaphoreType.DMA((count, 10)),
        pltpu.SemaphoreType.DMA((count, 10)),
        pltpu.SemaphoreType.DMA((count, 4)),
    ]
    return pl.pallas_call(
        functools.partial(backward_kernel, items, ring_size, depth),
        out_shape=(shape((micro, tokens, width), narrow),) + tuple(outs),
        in_specs=[IN_VMEM] * 3 + [ANY, ANY, IN_VMEM, ANY, ANY, ANY] + [ANY] * 3,
        out_specs=(IN_VMEM,) * 6,
        scratch_shapes=scratch,
        compiler_params=comm_params(collective),
    )(
        dcontext_part,
        seg_row,
        pack_part,
        qkv,
        context,
        stats,
        w_window,
        hidden_row,
        dresidual,
        *grads,
    )


def split_dot(left, right, left_dim, right_dim):
    high = left.astype(jnp.bfloat16)
    rest = (left - high.astype(jnp.float32)).astype(jnp.bfloat16)
    return contract(high, right, left_dim, right_dim) + contract(rest, right, left_dim, right_dim)


def retrieve_kernel(
    ring_size,
    dp_size,
    output,
    cotangent,
    seg_full,
    queries_all,
    hot_all,
    dout,
    embeddings,
    loss,
    query_grad,
    own,
    arrived,
    tables,
    everyone,
    asked,
    hot,
    wide_loss,
    dscore,
    turned,
    send_sem,
    recv_sem,
    ring_send,
    ring_recv,
):
    dp, blk, _ = place()
    ring = [(dp, lax.rem(blk + step, ring_size)) for step in range(1, ring_size)]
    members = [(lax.rem(dp + step, dp_size), blk) for step in range(1, dp_size)]
    greet(ring + members)
    micro, tokens, _ = output.shape
    many = own.shape[0] // micro
    seg_rows = seg_full.shape[0] // ring_size
    lane = lax.broadcasted_iota(jnp.int32, (many, tokens), 1)
    number = lax.broadcasted_iota(jnp.int32, (many, tokens), 0)
    selects = []
    for m in range(micro):
        here = seg_full[pl.ds(blk * seg_rows + m, 1)]
        there = seg_full[pl.ds(jnp.maximum(blk - 1, 0) * seg_rows + m, 1)]
        here = jnp.broadcast_to(here, (many, tokens))
        there = jnp.broadcast_to(there, (many, tokens))
        there = jnp.where(blk == 0, -1, there)
        before = jnp.where(lane == 0, pltpu.roll(there, 1, 1), pltpu.roll(here, 1, 1))
        chosen = (here != before) & (here == number)
        selects.append(jnp.where(chosen, 1.0, 0.0).astype(jnp.bfloat16))
        own[m * many : (m + 1) * many] = contract(selects[m], output[m], 1, 0).astype(jnp.bfloat16)
    copies = []
    for step, peer in enumerate(ring):
        copy = remote(own, arrived.at[step], ring_send.at[step], ring_recv.at[step], peer)
        copy.start()
        copies.append(copy)
    for d in range(dp_size):
        for m in range(micro):
            rows = slice((d * micro + m) * many, (d * micro + m + 1) * many)
            at = slice(d * many, (d + 1) * many)
            asked[m, at] = queries_all[rows]
            hot[m, at] = hot_all[rows]
    for copy in copies:
        copy.wait()
    total = own[...].astype(jnp.float32)
    for step in range(ring_size - 1):
        total = total + arrived[step].astype(jnp.float32)
    tables[dp] = total.astype(jnp.bfloat16)
    copies = []
    for step, peer in enumerate(members):
        copy = remote(tables.at[dp], tables.at[dp], send_sem.at[step], recv_sem.at[step], peer)
        copy.start()
        copies.append(copy)
    for m in range(micro):
        embeddings[m] = total[m * many : (m + 1) * many].astype(jnp.bfloat16)
    for copy in copies:
        copy.wait()
    for m in range(micro):
        for d in range(dp_size):
            everyone[m, d * many : (d + 1) * many] = tables[d, m * many : (m + 1) * many]
    mine = pl.ds(pl.multiple_of(dp * many, many), many)
    for m in range(micro):
        scores = contract(asked[m], everyone[m], 1, 1)
        peak = jnp.max(scores, axis=1, keepdims=True)
        log_total = peak + jnp.log(jnp.sum(jnp.exp(scores - peak), axis=1, keepdims=True))
        target = hot[m].astype(jnp.float32)
        value = log_total - jnp.sum(scores * target, axis=1, keepdims=True)
        wide_loss[...] = jnp.broadcast_to(value, wide_loss.shape)
        loss[m] = wide_loss[mine]
        slope = jnp.exp(scores - log_total) - target
        dscore[...] = slope
        turned[...] = slope.T
        query_grad[m] = split_dot(dscore[mine], everyone[m], 1, 0)
        embed_grad = split_dot(turned[mine], asked[m], 1, 0)
        high = embed_grad.astype(jnp.bfloat16)
        rest = (embed_grad - high.astype(jnp.float32)).astype(jnp.bfloat16)
        dout[m] = (
            cotangent[m].astype(jnp.float32)
            + contract(selects[m], high, 0, 0)
            + contract(selects[m], rest, 0, 0)
        )


def retrieve(output, cotangent, seg_full, queries_all, hot_all, ring_size, dp_size):
    micro, tokens, width = output.shape
    many = queries_all.shape[0] // (dp_size * micro)
    total = dp_size * many
    narrow, wide = jnp.bfloat16, jnp.float32
    shape = jax.ShapeDtypeStruct
    return pl.pallas_call(
        functools.partial(retrieve_kernel, ring_size, dp_size),
        out_shape=(
            shape((micro, tokens, width), wide),
            shape((micro, many, width), narrow),
            shape((micro, many, 128), wide),
            shape((micro, many, width), wide),
        ),
        in_specs=[IN_VMEM] * 5,
        out_specs=(IN_VMEM,) * 4,
        scratch_shapes=[
            pltpu.VMEM((micro * many, width), narrow),
            pltpu.VMEM((ring_size - 1, micro * many, width), narrow),
            pltpu.VMEM((dp_size, micro * many, width), narrow),
            pltpu.VMEM((micro, total, width), narrow),
            pltpu.VMEM((micro, total, width), narrow),
            pltpu.VMEM((micro, total, total), narrow),
            pltpu.VMEM((total, 128), wide),
            pltpu.VMEM((total, total), wide),
            pltpu.VMEM((total, total), wide),
            pltpu.SemaphoreType.DMA((dp_size,)),
            pltpu.SemaphoreType.DMA((dp_size,)),
            pltpu.SemaphoreType.DMA((ring_size,)),
            pltpu.SemaphoreType.DMA((ring_size,)),
        ],
        compiler_params=comm_params(4),
    )(output, cotangent, seg_full, queries_all, hot_all)


def gelu_and_slope(values):
    size = jnp.abs(values)
    step = 1.0 / (1.0 + (0.3275911 / math.sqrt(2.0)) * size)
    series = 0.5 * 1.061405429
    for factor in (-1.453152027, 1.421413741, -0.284496736, 0.254829592):
        series = series * step + 0.5 * factor
    bell = jnp.exp(-0.5 * values * values)
    tail = series * step * bell
    normal_cdf = jnp.where(values >= 0.0, 1.0 - tail, tail)
    slope = normal_cdf + values * bell * (1.0 / math.sqrt(2.0 * math.pi))
    return values * normal_cdf, slope


def fast_body(
    hidden_in,
    segment_ids,
    queries,
    targets,
    cotangent,
    query_weight,
    key_weight,
    value_weight,
    output_weight,
    query_bias,
    value_bias,
    output_bias,
    first_gain,
    first_shift,
    inner_weight,
    inner_bias,
    outer_weight,
    outer_bias,
    second_gain,
    second_shift,
):
    dp_size, ring_size = lax.axis_size("dp"), lax.axis_size("blk")
    dp, blk = lax.axis_index("dp"), lax.axis_index("blk")
    micro, row_count, block_tokens, width = hidden_in.shape
    row_queries = queries.shape[1]
    length = block_tokens * ring_size
    head_dim = width // HEADS
    spread = ring_size // micro
    own_heads = HEADS // spread
    tokens = micro * block_tokens
    wide = jnp.float32
    narrow = jnp.bfloat16

    vectors = (
        query_bias,
        value_bias,
        output_bias,
        first_gain,
        first_shift,
        outer_bias,
        second_gain,
        second_shift,
        inner_bias,
    )
    piece = vectors[0].shape[0]
    inner_piece = inner_bias.shape[0]
    group = own_heads * head_dim
    row_at, group_at = blk // spread, lax.rem(blk, spread) * group
    hidden_rows = hidden_in.reshape(micro, block_tokens, width)
    pack = jnp.concatenate(
        (
            jnp.pad(jnp.stack(vectors[:8]), ((0, 0), (0, inner_piece - piece))),
            jnp.pad(inner_bias[None], ((0, 7), (0, 0))),
        )
    )
    passages = dp_size * row_queries
    hot = (
        targets[:, :, None] == jnp.arange(passages, dtype=jnp.int32)[None, None, :]
    ).astype(narrow)
    seg_pack = jnp.pad(segment_ids.reshape(micro, block_tokens), ((0, 8 - micro), (0, 0)))
    shards = (
        query_weight,
        key_weight,
        value_weight,
        pack,
        hot.reshape(micro * row_queries, passages),
        queries.reshape(micro * row_queries, width),
        output_weight,
        inner_weight,
        outer_weight,
    )
    ways = (("x", "y"), ("y", "x"))
    items = []

    def add_item(source, target, row=0, rows=None, from_column=0, columns=None, to_column=0):
        shape = shards[source].shape
        items.append(
            {
                "source": source,
                "target": target,
                "row": row,
                "rows": rows or shape[0],
                "stride": shape[0],
                "from_column": from_column,
                "columns": columns or shape[1],
                "to_column": to_column,
                "route": ways[len(items) % 2],
            }
        )

    for index in range(3):
        add_item(index, 0, from_column=None, columns=group, to_column=index * group)
    add_item(3, 1)
    add_item(6, 4)
    for part in range(4):
        add_item(7, 5, from_column=part * width, columns=width, to_column=part * width)
        add_item(8, 6, row=part * piece, rows=piece)
    add_item(4, 2)
    add_item(5, 3)
    targets_out = [jax.ShapeDtypeStruct((width, 3 * group), narrow)] + [
        jax.ShapeDtypeStruct((dp_size * s.shape[0], s.shape[1]), s.dtype) for s in shards[3:]
    ]
    (
        w_window,
        pack_all,
        hot_all,
        queries_all,
        wo_full,
        w_inner,
        w_outer,
        seg_all,
        hidden_row,
        qkv,
        context,
        stats,
        context_t,
    ) = forward(shards, items, targets_out, seg_pack, hidden_rows, ring_size, head_dim)
    pack_rows = pack_all.reshape(dp_size, 16, inner_piece)
    eight = pack_rows[:, :8, :piece].transpose(1, 0, 2).reshape(8, width).astype(wide)
    bq_full, bv_full, bo_full, gain_one, shift_one, b_outer, gain_two, shift_two = eight
    b_inner = pack_rows[:, 8].reshape(-1).astype(wide)
    seg_row = (
        seg_all.reshape(ring_size, 8, block_tokens)[:, :micro]
        .transpose(1, 0, 2)
        .reshape(micro, 1, length)
    )
    seg_mine = lax.dynamic_slice(seg_row, (row_at, 0, 0), (1, 1, length)).reshape(1, length)

    flat_rows = hidden_in.reshape(tokens, width)
    attended = (
        jnp.einsum("met,ed->mtd", context_t, wo_full, preferred_element_type=wide).reshape(
            tokens, width
        )
        + bo_full
    )
    first_out, first_normed, first_factor = layer_norm(
        flat_rows.astype(wide) + attended, gain_one, shift_one
    )
    first_low = first_out.astype(narrow)
    inner_pre = jnp.dot(first_low, w_inner, preferred_element_type=wide) + b_inner
    active, slope = gelu_and_slope(inner_pre)
    active, slope = lax.optimization_barrier((active.astype(narrow), slope.astype(narrow)))
    outer_out = jnp.dot(active, w_outer, preferred_element_type=wide) + b_outer
    output, second_normed, second_factor = layer_norm(first_out + outer_out, gain_two, shift_two)
    output_low = output.astype(narrow)
    output_rows = output_low.reshape(micro, block_tokens, width)

    dout, embeddings, query_loss, query_grad = retrieve(
        output_rows,
        cotangent.reshape(micro, block_tokens, width),
        seg_all,
        queries_all,
        hot_all,
        ring_size,
        dp_size,
    )
    query_loss = query_loss[:, :, 0]
    dout = dout.reshape(tokens, width)
    gain_two_grad = jnp.sum(dout * second_normed, axis=0)
    shift_two_grad = jnp.sum(dout, axis=0)
    dsecond = norm_back(dout, second_normed, second_factor, gain_two)
    douter = dsecond.astype(narrow)
    outer_bias_grad = jnp.sum(douter.astype(wide), axis=0)
    outer_weight_grad = jnp.einsum(
        "nf,nd->fd", active, douter, preferred_element_type=wide
    ).astype(narrow)
    dactive = jnp.einsum("nd,fd->nf", douter, w_outer, preferred_element_type=wide)
    dinner = (dactive * slope.astype(wide)).astype(narrow)
    inner_bias_grad = jnp.sum(dinner.astype(wide), axis=0)
    inner_weight_grad = jnp.einsum(
        "nd,nf->df", first_low, dinner, preferred_element_type=wide
    ).astype(narrow)
    dfirst = dsecond + jnp.einsum("nf,df->nd", dinner, w_inner, preferred_element_type=wide)
    gain_one_grad = jnp.sum(dfirst * first_normed, axis=0)
    shift_one_grad = jnp.sum(dfirst, axis=0)
    dresidual = norm_back(dfirst, first_normed, first_factor, gain_one)
    dattended = dresidual.astype(narrow)
    output_bias_grad = jnp.sum(dattended.astype(wide), axis=0)
    datt_rows = dattended.reshape(micro, block_tokens, width)
    output_weight_grad = jnp.einsum(
        "met,mtd->ed", context_t, datt_rows, preferred_element_type=wide
    ).astype(narrow)
    dcontext_t = jnp.einsum(
        "mtd,ed->met", datt_rows, wo_full, preferred_element_type=wide
    ).astype(narrow)
    vector_grads = jnp.stack(
        (
            jnp.zeros((width,), wide),
            jnp.zeros((width,), wide),
            output_bias_grad,
            gain_one_grad,
            shift_one_grad,
            outer_bias_grad,
            gain_two_grad,
            shift_two_grad,
        )
    )
    grad_pack = jnp.pad(
        jnp.concatenate(
            (
                jnp.pad(
                    vector_grads.reshape(8, dp_size, piece).transpose(1, 0, 2),
                    ((0, 0), (0, 0), (0, inner_piece - piece)),
                ),
                inner_bias_grad.reshape(dp_size, 1, inner_piece),
            ),
            axis=1,
        ),
        ((0, 0), (0, 7), (0, 0)),
    ).reshape(dp_size * 16, inner_piece)
    grads = (outer_weight_grad, inner_weight_grad, output_weight_grad)
    grad_shapes = [grad.shape for grad in grads] + [(width, 3 * group), grad_pack.shape]
    sums = []

    def add_sum(source, row=0, rows=None, column=0, columns=None, widened=1):
        shape = grad_shapes[source]
        sums.append(
            {
                "source": source,
                "row": row,
                "rows": rows or shape[0] // dp_size,
                "stride": shape[0] // dp_size,
                "column": column,
                "columns": columns or shape[1],
                "widened": widened,
                "route": ways[len(sums) % 2],
            }
        )

    for part in range(4):
        add_sum(0, row=part * piece, rows=piece)
        add_sum(1, column=part * width, columns=width)
    add_sum(2)
    for index in range(3):
        add_sum(3, column=index * group, columns=group, widened=spread)
    add_sum(4)
    dhidden, d_outer, d_inner, d_wo, d_window, d_pack = backward(
        dcontext_t,
        seg_mine,
        grad_pack,
        (qkv, context, stats),
        w_window,
        hidden_row,
        dresidual.reshape(micro, block_tokens, width),
        grads,
        sums,
        ring_size,
        dp_size,
        head_dim,
        5,
    )
    d_outer, d_inner, d_wo, d_window, d_pack = (
        part.astype(wide) for part in (d_outer, d_inner, d_wo, d_window, d_pack)
    )
    d_wq, d_wk, d_wv = (d_window[:, i * width : (i + 1) * width] for i in range(3))
    d_bq, d_bv, d_bo, d_g1, d_s1, d_bu, d_g2, d_s2 = (d_pack[i, :piece] for i in range(8))
    d_bi = d_pack[8]
    shape = (micro, row_count, block_tokens, width)
    return (
        output_low.reshape(shape),
        embeddings,
        query_loss,
        query_grad,
        dhidden.reshape(shape),
        d_wq,
        d_wk,
        d_wv,
        d_wo,
        d_bq,
        d_bv,
        d_bo,
        d_g1,
        d_s1,
        d_inner,
        d_bi,
        d_outer,
        d_bu,
        d_g2,
        d_s2,
    )


def solution(mesh):
    in_specs = (
        P(None, "dp", "blk", None),
        P(None, "dp", "blk"),
        P(None, "dp", None),
        P(None, "dp"),
        P(None, "dp", "blk", None),
        P("dp", None),
        P("dp", None),
        P("dp", None),
        P("dp", None),
        P("dp"),
        P("dp"),
        P("dp"),
        P("dp"),
        P("dp"),
        P("dp", None),
        P("dp"),
        P("dp", None),
        P("dp"),
        P("dp"),
        P("dp"),
    )
    out_specs = (
        P(None, "dp", "blk", None),
        P(None, "dp", None),
        P(None, "dp"),
        P(None, "dp", None),
        P(None, "dp", "blk", None),
        P("dp", None),
        P("dp", None),
        P("dp", None),
        P("dp", None),
        P("dp"),
        P("dp"),
        P("dp"),
        P("dp"),
        P("dp"),
        P("dp", None),
        P("dp"),
        P("dp", None),
        P("dp"),
        P("dp"),
        P("dp"),
    )
    fast = mesh.shape["dp"] == 8 and mesh.shape["blk"] == 4
    body = fast_body if fast else ring_body
    return jax.shard_map(body, mesh=mesh, in_specs=in_specs, out_specs=out_specs, check_vma=False)
```

profile of v0, /device:TPU:0, one launch (start us, length us, event | category | flops | bytes accessed | tf_op | source)
XLA Modules:
  0.0 279.1 jit_solution(17805460947655789626)
XLA Ops:
  0.7 0.8 eq.16
  2.1 0.7 copy.58
  2.8 0.8 stack.59
  5.5 1.2 bitcast_convert_fusion.1
  6.7 78.0 %shard_map.347 = (bf16[768,1152]{1,0:T(8,128)(2,1)}, bf16[128,384]{1,0:T(8,128)(2,1)}, bf16[256,128]{1,0:T(8,128)(2,1)}, bf16[256,768]{1,0:T(8,128)(2,1)}, bf16[...) custom-call(bf16[96,768]{1,0:T(8,128)(2,1)} %refs_0_.1, ...), custom_call_target="tpu_custom_call" | custom-call | tf_op jit(solution)/shard_map/pallas_call | solution.py:828
  84.7 0.8 slice.72
  86.1 0.8 slice_convert_fusion
  86.9 0.7 convert_bitcast_fusion
  88.1 2.5 fusion.15
  91.4 2.0 copy-done.9
  93.4 8.8 %fusion.5 = (bf16[512,3072]{1,0:T(8,128)(2,1)}, bf16[512,3072]{1,0:T(8,128)(2,1)S(1)}) fusion(f32[3072]{0:T(1024)S(1)} %bitcast.131, bf16[768,3072]{1,0:T(8,128)(2,1)S(1)} %copy-done.9, f32[512,768]{1,0:T(8,128)S(1)} %fusion.9, f32[768]{0:T(1024)S(1)} %add.140, f32[768]{0:T(1024)S(1)} %mul.154), kind=kOutput, calls=%fused_computation.7 | convolution fusion | flops 2457993216 | bytes 12601344 | tf_op jit(solution)/shard_map/dot_general | solution.py:1686
  102.2 2.7 fusion.28
  105.3 1.2 add_convert_fusion
  106.5 17.7 %shard_map.348 = (f32[2,256,768]{2,1,0:T(8,128)}, bf16[2,16,768]{2,1,0:T(8,128)(2,1)}, f32[2,16,128]{2,1,0:T(8,128)}, f32[2,16,768]{2,1,0:T(8,128)}) custom-call(bf16[2,256,768]{2,1,0:T(8,128)(2,1)} %bitcast.118, bf16[2,256,768]{2,1,0:T(8,128)(2,1)} %bitcast.122, s32[32,256]{1,0:T(8,128)} %get-tuple-element.51.seg_full, ...), custom_call_target="tpu_custom_call" | custom-call | tf_op jit(solution)/shard_map/pallas_call | solution.py:1504
  124.1 1.5 slice_reduce_fusion
  125.6 1.6 fusion.26
  128.5 6.0 %convert_reduce_fusion = (f32[3072]{0:T(1024)S(1)}, bf16[512,3072]{1,0:T(8,128)(2,1)S(1)}) fusion(bf16[512,3072]{1,0:T(8,128)(2,1)} %get-tuple-element.58, bf16[3072,768]{1,0:T(8,128)(2,1)} %get-tuple-element.50, f32[512,768]{1,0:T(8,128)S(1)} %get-tuple-element.125), kind=kOutput, calls=%fused_computation.8 | convolution fusion | flops 2424173568 | bytes 12595200 | tf_op jit(solution)/shard_map/nd,fd->nf/dot_general | solution.py:1713
  134.6 3.0 %multiply_reduce_fusion = (f32[768]{0:T(1024)S(1)}, f32[512]{0:T(512)S(1)}, f32[512]{0:T(512)S(1)}, f32[768]{0:T(1024)S(1)}, f32[512,768]{1,0:T(8,128)S(1)}) fusion(f32[512,768]{1,0:T(8,128)S(1)} %copy-done.3, f32[768]{0:T(1024)S(1)} %mul.154, f32[512,768]{1,0:T(8,128)S(1)} %get-tuple-element.125, bf16[512,3072]{1,0:T(8,128)(2,1)S(1)} %get-tuple-element.150, ...), kind=kOutput, calls=%fused_computation.23 | convolution fusion | flops 2419062272 | bytes 12596224 | tf_op jit(solution)/shard_map/nf,df->nd/dot_general | solution.py:1719
  137.6 4.3 %convolution_convert_fusion.1.refs_9_ = bf16[3072,768]{1,0:T(8,128)(2,1)} fusion(bf16[512,3072]{1,0:T(8,128)(2,1)S(1)} %copy-done.15, f32[512,768]{1,0:T(8,128)S(1)} %get-tuple-element.125), kind=kOutput, calls=%fused_computation.12 | convolution fusion | flops 2418671616 | bytes 9437184 | tf_op jit(solution)/shard_map/nf,nd->fd/dot_general | solution.py:1710
  142.1 1.6 convert_reduce_fusion.2
  143.7 0.9 copy-done.13
  144.6 4.8 %convolution_convert_fusion.refs_10_ = bf16[768,3072]{1,0:T(8,128)(2,1)} fusion(bf16[512,3072]{1,0:T(8,128)(2,1)S(1)} %copy-done.13, f32[512,768]{1,0:T(8,128)S(1)} %copy-done.3, f32[768]{0:T(1024)S(1)} %add.140, f32[768]{0:T(1024)S(1)} %mul.154), kind=kOutput, calls=%fused_computation.11 | convolution fusion | flops 2419458048 | bytes 9443328 | tf_op jit(solution)/shard_map/nd,nf->df/dot_general | solution.py:1716
  149.5 1.7 fusion.11.refs_0_
  151.2 1.8 bitcast_convert_fusion.refs_11_
  153.1 0.7 pad.24
  153.8 115.1 %shard_map.349 = (bf16[2,256,768]{2,1,0:T(8,128)(2,1)}, bf16[384,768]{1,0:T(8,128)(2,1)}, bf16[96,3072]{1,0:T(8,128)(2,1)}, bf16[96,768]{1,0:T(8,128)(2,1)}, bf1...) custom-call(bf16[2,768,256]{2,1,0:T(8,128)(2,1)} %fusion.11.refs_0_, s32[1,1024]{1,0:T(1,128)} %dynamic-slice_bitcast_fusion.refs_1_, ...), custom_call_target="tpu_custom_call" | custom-call | tf_op jit(solution)/shard_map/pallas_call | solution.py:1373
  268.9 0.8 convert_element_type.127
  270.8 1.6 convert_element_type.126
  272.5 2.0 fusion.27
  274.6 1.1 convert_element_type.128
  275.7 1.1 convert_element_type.129
  278.0 0.9 copy.64
  (82 shorter events, 8.9 us)
Async XLA Ops:
  6.7 81.4 %copy-start.1 = (bf16[2,1,256,768]{3,2,1,0:T(8,128)(2,1)S(1)}, bf16[2,1,256,768]{3,2,1,0:T(8,128)(2,1)}, u32[]{:S(2)}) copy-start(bf16[2,1,256,768]{3,2,1,0:T(8,128)(2,1)} %param.20) | copy-start | bytes 2359300
  91.1 2.3 copy-start.9
  91.1 11.1 %slice-start.2 = ((s8[4718592]{0:T(1024)(128)(4,1)}), s8[4194304]{0:T(1024)(128)(4,1)S(1)}, s32[]{:S(2)}) async-start(s8[4718592]{0:T(1024)(128)(4,1)} %bitcast.148), calls=%async_computation.2 | async-start | bytes 8388608
  93.4 8.8 %copy-start.2 = (f32[512,768]{1,0:T(8,128)}, f32[512,768]{1,0:T(8,128)S(1)}, u32[]{:S(2)}) copy-start(f32[512,768]{1,0:T(8,128)S(1)} %fusion.9) | copy-start | bytes 4718596
  93.4 8.8 %slice-start.3 = ((s8[4718592]{0:T(1024)(128)(4,1)}), s8[524288]{0:T(1024)(128)(4,1)S(1)}, s32[]{:S(2)}) async-start(s8[4718592]{0:T(1024)(128)(4,1)} %bitcast.148), calls=%async_computation.3 | async-start | bytes 1048576
  102.2 2.7 copy-start.14
  124.1 3.2 %copy-start = (f32[2,256,768]{2,1,0:T(8,128)S(1)}, f32[2,256,768]{2,1,0:T(8,128)}, u32[]{:S(2)}) copy-start(f32[2,256,768]{2,1,0:T(8,128)} %get-tuple-element.57) | copy-start | bytes 4718596
  128.0 6.5 %slice-start = ((s8[4718592]{0:T(1024)(128)(4,1)}), s8[4194304]{0:T(1024)(128)(4,1)S(1)}, s32[]{:S(2)}) async-start(s8[4718592]{0:T(1024)(128)(4,1)} %bitcast.146), calls=%async_computation | async-start | bytes 8388608
  128.5 6.0 %copy-start.3 = (f32[512,768]{1,0:T(8,128)S(1)}, f32[512,768]{1,0:T(8,128)}, u32[]{:S(2)}) copy-start(f32[512,768]{1,0:T(8,128)} %copy-done.2) | copy-start | bytes 4718596
  128.5 6.0 %slice-start.1 = ((s8[4718592]{0:T(1024)(128)(4,1)}), s8[524288]{0:T(1024)(128)(4,1)S(1)}, s32[]{:S(2)}) async-start(s8[4718592]{0:T(1024)(128)(4,1)} %bitcast.146), calls=%async_computation.1 | async-start | bytes 1048576
  134.5 3.0 %copy-start.12 = (bf16[512,3072]{1,0:T(8,128)(2,1)}, bf16[512,3072]{1,0:T(8,128)(2,1)S(1)}, u32[]{:S(2)}) copy-start(bf16[512,3072]{1,0:T(8,128)(2,1)S(1)} %get-tuple-element.150) | copy-start | bytes 9437188
  134.6 3.0 %copy-start.15 = (bf16[512,3072]{1,0:T(8,128)(2,1)S(1)}, bf16[512,3072]{1,0:T(8,128)(2,1)}, u32[]{:S(2)}) copy-start(bf16[512,3072]{1,0:T(8,128)(2,1)} %copy-done.14) | copy-start | bytes 9437188
  142.1 2.5 copy-start.13
  144.6 4.9 %copy-start.10 = (bf16[768,768]{1,0:T(8,128)(2,1)S(1)}, bf16[768,768]{1,0:T(8,128)(2,1)}, u32[]{:S(2)}) copy-start(bf16[768,768]{1,0:T(8,128)(2,1)} %get-tuple-element.46) | copy-start | bytes 3538948
  149.5 1.7 copy-start.11
  268.9 5.6 %copy-start.6 = (bf16[96,3072]{1,0:T(8,128)(2,1)S(1)}, bf16[96,3072]{1,0:T(8,128)(2,1)}, u32[]{:S(2)}) copy-start(bf16[96,3072]{1,0:T(8,128)(2,1)} %get-tuple-element.68) | copy-start | bytes 1769476
  272.5 3.2 %copy-start.5 = (bf16[384,768]{1,0:T(8,128)(2,1)S(1)}, bf16[384,768]{1,0:T(8,128)(2,1)}, u32[]{:S(2)}) copy-start(bf16[384,768]{1,0:T(8,128)(2,1)} %get-tuple-element.69) | copy-start | bytes 1769476
  274.5 2.2 copy-start.8
  274.5 2.8 %copy-start.7 = (f32[2,16,768]{2,1,0:T(8,128)S(1)}, f32[2,16,768]{2,1,0:T(8,128)}, u32[]{:S(2)}) copy-start(f32[2,16,768]{2,1,0:T(8,128)} %get-tuple-element.176) | copy-start | bytes 294916
  274.5 3.5 %copy-start.4 = (bf16[2,256,768]{2,1,0:T(8,128)(2,1)S(1)}, bf16[2,256,768]{2,1,0:T(8,128)(2,1)}, u32[]{:S(2)}) copy-start(bf16[2,256,768]{2,1,0:T(8,128)(2,1)} %get-tuple-element.64) | copy-start | bytes 2359300
where the time goes:
time: 284 us; the launch traced here: 279 us
  Pallas kernels  211 us (74%)
  matrix products  35.6 us (13%)
  local copies, waits for them, and re-layouts  16.4 us (6%)
  other arithmetic  15.2 us (5%)
    pallas_call x1, Pallas kernels, backward(): pl.pallas_call(functools.partial(backward_kernel, items, ring_size, depth...  115 us
    pallas_call x1, Pallas kernels, forward(): pl.pallas_call(functools.partial(forward_kernel, items, ring_size, depth,...  78 us
    pallas_call x1, Pallas kernels, retrieve(): pl.pallas_call(functools.partial(retrieve_kernel, ring_size, dp_size), ou...  17.7 us
    dot_general x1, matrix products, fast_body(): jnp.dot(first_low, w_inner, preferred_element_type=wide) + b_inner  8.79 us
    dot_general x1, matrix products, fast_body(): jnp.einsum('nd,fd->nf', douter, w_outer, preferred_element_type=wide)  5.98 us
    unnamed x48, local copies, waits for them, and re-layouts  5.78 us

commit v1 on v0

--- a/solution.py
+++ b/solution.py
@@ -501,9 +501,18 @@
 def forward_kernel(items, ring_size, depth, sources, places, *refs):
     shards, seg_shard, hidden = refs[:sources], refs[sources], refs[sources + 1]
     outs = refs[sources + 2 :]
-    fulls = outs[:places]
-    seg_full, hidden_row, qkv, context, stats, context_t = outs[places : places + 6]
+    w_window_out, hidden_row_out, qkv_out, context_out = (
+        outs[0],
+        outs[places + 1],
+        outs[places + 2],
+        outs[places + 3],
+    )
+    seg_full, stats, context_t = outs[places], outs[places + 4], outs[places + 5]
     (
+        w_window,
+        hidden_row,
+        qkv,
+        context,
         hidden_full,
         low,
         seg_line,
@@ -519,8 +528,17 @@
         head_send,
         head_recv,
         local_sem,
+        store_sem,
     ) = outs[places + 6 :]
-    w_window, pack_full = fulls[0], fulls[1]
+    fulls = (w_window,) + tuple(outs[1:places])
+    pack_full = fulls[1]
+    stores = []
+
+    def store(source, target):
+        copy = pltpu.make_async_copy(source, target, store_sem.at[len(stores)])
+        copy.start()
+        stores.append(copy)
+
     dp, blk, bits = place()
     sibling = across(dp, blk, bits, "c")
     ring = [(dp, lax.rem(blk + step, ring_size)) for step in range(1, ring_size)]
@@ -700,6 +718,7 @@
     seg_col = columns_of(seg_line[...])
     for item in early:
         all_here(item)
+    store(w_window, w_window_out)
     pack_turned = pack_full[...].astype(jnp.float32).T
     piece = width // (pack_full.shape[0] // 16)
     lane = lax.broadcasted_iota(jnp.int32, (piece, pack_full.shape[0]), 1)
@@ -752,6 +771,8 @@
                 tick()
         project_at(distance)
 
+    store(hidden_row, hidden_row_out)
+    store(qkv, qkv_out)
     copies = []
 
     def head_rows(part, head):
@@ -791,6 +812,7 @@
         else:
             target[...] = low[:, span]
         tick(2)
+    store(context, context_out)
     tick(len(late) + 2 * LAG - tick_of[0])
     for item in late:
         all_here(item)
@@ -799,6 +821,8 @@
             inbound[item, slot].wait_send()
     for copy in copies:
         copy.wait_send()
+    for copy in stores:
+        copy.wait()
     for step, peer in enumerate(ring):
         remote(target, target, head_send.at[0], head_recv.at[step + 1], peer).wait_recv()
     for m in range(micro):
@@ -837,8 +861,14 @@
             shape((micro, width, tokens), jnp.bfloat16),
         ),
         in_specs=[IN_VMEM] * (count + 2),
-        out_specs=(IN_VMEM, IN_VMEM) + (ANY,) * (len(targets) - 2) + (IN_VMEM,) * 6,
+        out_specs=(ANY, IN_VMEM)
+        + (ANY,) * (len(targets) - 2)
+        + (IN_VMEM, ANY, ANY, ANY, IN_VMEM, IN_VMEM),
         scratch_shapes=[
+            pltpu.VMEM((width, 3 * group), jnp.bfloat16),
+            pltpu.VMEM((length, width), jnp.bfloat16),
+            pltpu.VMEM((3 * group, length), jnp.bfloat16),
+            pltpu.VMEM((group, length), jnp.float32),
             pltpu.VMEM((micro, length, width), jnp.bfloat16),
             pltpu.VMEM((group, length), jnp.bfloat16),
             pltpu.VMEM((1, length), jnp.float32),
@@ -854,6 +884,7 @@
             pltpu.SemaphoreType.DMA((ring_size,)),
             pltpu.SemaphoreType.DMA((ring_size,)),
             pltpu.SemaphoreType.DMA((len(items),)),
+            pltpu.SemaphoreType.DMA((4,)),
         ],
         compiler_params=comm_params(1),
     )(*shards, segments, hidden)
@@ -865,7 +896,7 @@
     )
 
 
-LAG, AHEAD = 2, 3
+LAG, AHEAD = 3, 3
 
 
 def added(left, right):
@@ -883,11 +914,12 @@
         w_window_out,
         hidden_row_out,
         dresidual_out,
-        outer_grad,
+        active_out,
+        douter,
         inner_grad,
         output_grad,
-    ) = refs[:12]
-    dhidden, d_outer, d_inner, d_output, d_window, d_pack = refs[12:18]
+    ) = refs[:13]
+    dhidden, d_outer, d_inner, d_output, d_window, d_pack = refs[13:19]
     (
         qkv,
         context,
@@ -896,16 +928,20 @@
         dresidual,
         dcontext,
         dwindow,
-        parts,
-        passed,
+        pool,
         arrived,
         window_grad,
         pack_sum,
         pack_low,
-        own,
-        from_core,
-        from_first,
-        from_second,
+        outer_parts,
+        own_big,
+        own_small,
+        core_big,
+        core_small,
+        first_big,
+        first_small,
+        second_big,
+        second_small,
         ring_one,
         ring_two,
         load_sem,
@@ -916,8 +952,12 @@
         send_sem,
         recv_sem,
         local_sem,
-    ) = refs[18:]
-    grads = (outer_grad, inner_grad, output_grad, window_grad, pack_low)
+    ) = refs[19:]
+    own, from_core = (own_big, own_small), (core_big, core_small)
+    from_first, from_second = (first_big, first_small), (second_big, second_small)
+    big = own_big.shape[0]
+    parts, passed_at = pool, ring_size
+    grads = (None, inner_grad, output_grad, window_grad, pack_low)
     outs = (d_outer, d_inner, d_output, d_window, d_pack)
     count = len(items)
     dp, blk, bits = place()
@@ -950,6 +990,16 @@
         copy = pltpu.make_async_copy(source, target, load_sem.at[index])
         copy.start()
         loads.append(copy)
+
+    for half in range(micro):
+        for part in range(ring_size):
+            copy = pltpu.make_async_copy(
+                active_out.at[pl.ds(half * tokens, tokens), pl.ds(part * width, width)],
+                pool.at[part * micro + half],
+                load_sem.at[len(loads)],
+            )
+            copy.start()
+            loads.append(copy)
 
     head_copies = []
     def send_head(head):
@@ -979,9 +1029,10 @@
             pl.ds(spec["column"], spec["columns"]),
         ]
 
-    def cut(buffer, item, *index):
+    def cut(buffers, item, *index):
         spec = items[item]
-        return buffer.at[(item,) + index + (pl.ds(0, spec["rows"]), pl.ds(0, spec["columns"]))]
+        buffer, at = (buffers[0], item) if item < big else (buffers[1], item - big)
+        return buffer.at[(at,) + index + (pl.ds(0, spec["rows"]), pl.ds(0, spec["columns"]))]
 
     def wide_cut(buffer, item, *index):
         spec = items[item]
@@ -1011,6 +1062,12 @@
         for f in range(2):
             for s in range(2):
                 slot = 2 * f + s
+                if items[item]["source"] == 0:
+                    rows = pl.ds(items[item]["row"], items[item]["rows"])
+                    ahead, behind = (f, s) if axes[0] == "x" else (s, f)
+                    part = outer_parts.at[ahead, behind, rows]
+                    go(part, cut(from_core, item, f, s), item, slot, sibling)
+                    continue
                 go(
                     block(item, owner_of(1 - bits["c"], axes, f, s)),
                     cut(from_core, item, f, s),
@@ -1031,7 +1088,8 @@
         kept = bits[axes[0]]
         for slot in range(4):
             flying[item, slot].wait_recv()
-            flying[item, "own", slot].wait()
+            if items[item]["source"] != 0:
+                flying[item, "own", slot].wait()
         for stays, f in ((False, 1 - kept), (True, kept)):
             for s in range(2):
                 part = cut(own, item, f, s)
@@ -1058,16 +1116,15 @@
         flying[item, 6].wait_recv()
         total = added(cut(own, item, f, s)[...], cut(from_second, item)[...])
         if spec["widened"] > 1:
-            wide_cut(ring_one, item, 0)[...] = jnp.zeros(
-                (spec["rows"], spec["columns"] * spec["widened"]), jnp.bfloat16
-            )
             at = pl.multiple_of(group_at * spec["columns"], 128)
-            ring_one[item, 0, pl.ds(0, spec["rows"]), pl.ds(at, spec["columns"])] = total
+            part = ring_two.at[item, 0, pl.ds(0, spec["rows"]), pl.ds(at, spec["columns"])]
+            part[...] = total
+            flying[item, 7] = copier(part, part, item, 7, partner)
         else:
             wide_cut(ring_one, item, 0)[...] = total
-        flying[item, 7] = copier(
-            wide_cut(ring_one, item, 0), wide_cut(ring_one, item, 1), item, 7, partner
-        )
+            flying[item, 7] = copier(
+                wide_cut(ring_one, item, 0), wide_cut(ring_one, item, 1), item, 7, partner
+            )
         flying[item, 8] = copier(
             wide_cut(ring_two, item, 0), wide_cut(ring_two, item, 1), item, 8, facing
         )
@@ -1081,8 +1138,11 @@
         @pl.when(is_middle)
         def _():
             flying[item, 7].wait_recv()
-            part = wide_cut(ring_two, item, 0)
-            part[...] = added(wide_cut(ring_one, item, 0)[...], wide_cut(ring_one, item, 1)[...])
+            if items[item]["widened"] == 1:
+                part = wide_cut(ring_two, item, 0)
+                part[...] = added(
+                    wide_cut(ring_one, item, 0)[...], wide_cut(ring_one, item, 1)[...]
+                )
             flying[item, 8].start()
 
     def across_middle(item):
@@ -1151,12 +1211,44 @@
         dwindow[rows(1), :] = dkey_sum.astype(jnp.bfloat16)
         dwindow[rows(2), :] = dvalue_sum.astype(jnp.bfloat16)
 
+    def outer_block(core, x_bit, y_bit):
+        stride = width // 2
+        rows = pl.ds(pl.multiple_of(core * stride, 128), stride)
+        part = x_bit + 2 * y_bit
+        total = sum(
+            contract(
+                pool[part * micro + half, :, rows],
+                douter[half * tokens : (half + 1) * tokens, :],
+                0,
+                0,
+            )
+            for half in range(micro)
+        )
+        return total.astype(jnp.bfloat16)
+
+    def outer_work(step):
+        x_bit, y_bit = step % 4 // 2, step % 2
+        if step < 4:
+            outer_parts[x_bit, y_bit] = outer_block(1 - bits["c"], x_bit, y_bit)
+            return
+        values = outer_block(bits["c"], x_bit, y_bit)
+        for item, spec in enumerate(items):
+            if spec["source"] == 0:
+                f, s = (x_bit, y_bit) if spec["route"][0] == "x" else (y_bit, x_bit)
+                cut(own, item, f, s)[...] = values[spec["row"] : spec["row"] + spec["rows"]]
+
     loads[0].wait()
     loads[1].wait()
     for head in range(heads):
         if head + 2 < heads:
             send_head(head + 2)
         one_head(head)
+        if head == 0:
+            for copy in loads[5:]:
+                copy.wait()
+        if head < 4:
+            outer_work(2 * head)
+            outer_work(2 * head + 1)
         tick()
     loads[2].wait()
     loads[3].wait()
@@ -1212,8 +1304,8 @@
                 @pl.when(goes & owns(m))
                 def _():
                     arrival(m, side, distance).wait_recv()
-                    passed[side, distance - 1] = added(parts[target], arrived[m, side, distance])
-                    hop(passed.at[side, distance - 1], m, side, distance).start()
+                    pool[passed_at + 2 * side + distance - 1] = added(parts[target], arrived[m, side, distance])
+                    hop(pool.at[passed_at + 2 * side + distance - 1], m, side, distance).start()
 
                 @pl.when(goes & jnp.logical_not(owns(m)))
                 def _():
@@ -1320,6 +1412,8 @@
     w_window,
     hidden_row,
     dresidual,
+    active,
+    douter,
     grads,
     items,
     ring_size,
@@ -1338,7 +1432,8 @@
     piece = (rows, columns)
     narrow = jnp.bfloat16
     shape = jax.ShapeDtypeStruct
-    outs = [shape((grad.shape[0] // dp_size, grad.shape[1]), narrow) for grad in grads]
+    outs = [shape((active.shape[1] // dp_size, width), narrow)]
+    outs += [shape((grad.shape[0] // dp_size, grad.shape[1]), narrow) for grad in grads]
     outs.append(shape((width // dp_size, 3 * width), narrow))
     outs.append(shape((pack_part.shape[0] // dp_size, pack_part.shape[1]), narrow))
     scratch = [
@@ -1349,19 +1444,24 @@
         pltpu.VMEM(dresidual.shape, jnp.float32),
         pltpu.VMEM((group, length), narrow),
         pltpu.VMEM(qkv.shape, narrow),
-        pltpu.VMEM((ring_size, tokens, width), narrow),
-        pltpu.VMEM((2, ring_size - 2, tokens, width), narrow),
+        pltpu.VMEM((2 * ring_size, tokens, width), narrow),
         pltpu.VMEM((micro, 2, ring_size - 1, tokens, width), narrow),
         pltpu.VMEM((width, 3 * group), narrow),
         pltpu.VMEM(pack_part.shape, jnp.float32),
         pltpu.VMEM(pack_part.shape, narrow),
     ]
+    big = sum(item["source"] < 3 for item in items)
     scratch += [
-        pltpu.VMEM((count,) + lead + piece, narrow)
-        for lead in ((2, 2), (2, 2), (2,), (), (2,), (2,))
+        pltpu.VMEM((2, 2, active.shape[1] // dp_size, width), narrow),
     ]
+    for lead in ((2, 2), (2, 2), (2,), ()):
+        scratch += [
+            pltpu.VMEM((big,) + lead + (rows, width), narrow),
+            pltpu.VMEM((count - big,) + lead + (rows, group), narrow),
+        ]
+    scratch += [pltpu.VMEM((count, 2) + piece, narrow)] * 2
     scratch += [
-        pltpu.SemaphoreType.DMA((5,)),
+        pltpu.SemaphoreType.DMA((5 + 2 * ring_size,)),
         pltpu.SemaphoreType.DMA((heads, ring_size)),
         pltpu.SemaphoreType.DMA((heads, ring_size)),
         pltpu.SemaphoreType.DMA((micro, 2, ring_size)),
@@ -1373,7 +1473,7 @@
     return pl.pallas_call(
         functools.partial(backward_kernel, items, ring_size, depth),
         out_shape=(shape((micro, tokens, width), narrow),) + tuple(outs),
-        in_specs=[IN_VMEM] * 3 + [ANY, ANY, IN_VMEM, ANY, ANY, ANY] + [ANY] * 3,
+        in_specs=[IN_VMEM] * 3 + [ANY, ANY, IN_VMEM, ANY, ANY, ANY, ANY, IN_VMEM, ANY, ANY],
         out_specs=(IN_VMEM,) * 6,
         scratch_shapes=scratch,
         compiler_params=comm_params(collective),
@@ -1387,6 +1487,8 @@
         w_window,
         hidden_row,
         dresidual,
+        active,
+        douter,
         *grads,
     )
 
@@ -1405,7 +1507,12 @@
     seg_full,
     queries_all,
     hot_all,
-    dout,
+    normed,
+    factor,
+    gain,
+    dsecond,
+    douter,
+    sums,
     embeddings,
     loss,
     query_grad,
@@ -1488,14 +1595,32 @@
         embed_grad = split_dot(turned[mine], asked[m], 1, 0)
         high = embed_grad.astype(jnp.bfloat16)
         rest = (embed_grad - high.astype(jnp.float32)).astype(jnp.bfloat16)
-        dout[m] = (
+        dout = (
             cotangent[m].astype(jnp.float32)
             + contract(selects[m], high, 0, 0)
             + contract(selects[m], rest, 0, 0)
         )
-
-
-def retrieve(output, cotangent, seg_full, queries_all, hot_all, ring_size, dp_size):
+        scaled = dout * gain[...]
+        product = dout * normed[m]
+        inner_term = (
+            scaled
+            - jnp.mean(scaled, axis=1, keepdims=True)
+            - normed[m] * jnp.mean(scaled * normed[m], axis=1, keepdims=True)
+        ) * factor[m]
+        dsecond[m] = inner_term
+        rounded = inner_term.astype(jnp.bfloat16)
+        douter[m] = rounded
+        for row, values in enumerate((product, dout, rounded.astype(jnp.float32))):
+            line = jnp.sum(values, axis=0, keepdims=True)
+            if m == 0:
+                sums[row : row + 1] = line
+            else:
+                sums[row : row + 1] += line
+
+
+def retrieve(
+    output, cotangent, seg_full, queries_all, hot_all, normed, factor, gain, ring_size, dp_size
+):
     micro, tokens, width = output.shape
     many = queries_all.shape[0] // (dp_size * micro)
     total = dp_size * many
@@ -1505,12 +1630,14 @@
         functools.partial(retrieve_kernel, ring_size, dp_size),
         out_shape=(
             shape((micro, tokens, width), wide),
+            shape((micro, tokens, width), narrow),
+            shape((8, width), wide),
             shape((micro, many, width), narrow),
             shape((micro, many, 128), wide),
             shape((micro, many, width), wide),
         ),
-        in_specs=[IN_VMEM] * 5,
-        out_specs=(IN_VMEM,) * 4,
+        in_specs=[IN_VMEM] * 8,
+        out_specs=(IN_VMEM,) * 6,
         scratch_shapes=[
             pltpu.VMEM((micro * many, width), narrow),
             pltpu.VMEM((ring_size - 1, micro * many, width), narrow),
@@ -1527,7 +1654,7 @@
             pltpu.SemaphoreType.DMA((ring_size,)),
         ],
         compiler_params=comm_params(4),
-    )(output, cotangent, seg_full, queries_all, hot_all)
+    )(output, cotangent, seg_full, queries_all, hot_all, normed, factor, gain)
 
 
 def gelu_and_slope(values):
@@ -1691,25 +1818,22 @@
     output_low = output.astype(narrow)
     output_rows = output_low.reshape(micro, block_tokens, width)
 
-    dout, embeddings, query_loss, query_grad = retrieve(
+    dsecond, douter, second_sums, embeddings, query_loss, query_grad = retrieve(
         output_rows,
         cotangent.reshape(micro, block_tokens, width),
         seg_all,
         queries_all,
         hot_all,
+        second_normed.reshape(micro, block_tokens, width),
+        second_factor.reshape(micro, block_tokens, 1),
+        gain_two.reshape(1, width),
         ring_size,
         dp_size,
     )
     query_loss = query_loss[:, :, 0]
-    dout = dout.reshape(tokens, width)
-    gain_two_grad = jnp.sum(dout * second_normed, axis=0)
-    shift_two_grad = jnp.sum(dout, axis=0)
-    dsecond = norm_back(dout, second_normed, second_factor, gain_two)
-    douter = dsecond.astype(narrow)
-    outer_bias_grad = jnp.sum(douter.astype(wide), axis=0)
-    outer_weight_grad = jnp.einsum(
-        "nf,nd->fd", active, douter, preferred_element_type=wide
-    ).astype(narrow)
+    dsecond = dsecond.reshape(tokens, width)
+    douter = douter.reshape(tokens, width)
+    gain_two_grad, shift_two_grad, outer_bias_grad = second_sums[:3]
     dactive = jnp.einsum("nd,fd->nf", douter, w_outer, preferred_element_type=wide)
     dinner = (dactive * slope.astype(wide)).astype(narrow)
     inner_bias_grad = jnp.sum(dinner.astype(wide), axis=0)
@@ -1754,8 +1878,9 @@
         ),
         ((0, 0), (0, 7), (0, 0)),
     ).reshape(dp_size * 16, inner_piece)
-    grads = (outer_weight_grad, inner_weight_grad, output_weight_grad)
-    grad_shapes = [grad.shape for grad in grads] + [(width, 3 * group), grad_pack.shape]
+    grads = (inner_weight_grad, output_weight_grad)
+    grad_shapes = [(inner_bias.shape[0] * dp_size, width)]
+    grad_shapes += [grad.shape for grad in grads] + [(width, 3 * group), grad_pack.shape]
     sums = []
 
     def add_sum(source, row=0, rows=None, column=0, columns=None, widened=1):
@@ -1774,9 +1899,10 @@
         )
 
     for part in range(4):
-        add_sum(0, row=part * piece, rows=piece)
         add_sum(1, column=part * width, columns=width)
     add_sum(2)
+    for part in range(4):
+        add_sum(0, row=part * piece, rows=piece)
     for index in range(3):
         add_sum(3, column=index * group, columns=group, widened=spread)
     add_sum(4)
@@ -1788,6 +1914,8 @@
         w_window,
         hidden_row,
         dresidual.reshape(micro, block_tokens, width),
+        active,
+        douter,
         grads,
         sums,
         ring_size,

time: 284 us -> 280 us (0.986)
  matrix products: 35.6 us -> 31.9 us
    dot_general x1 -> x0, matrix products: 4.32 us -> none  [fast_body(): jnp.einsum('nf,nd->fd', active, douter, preferred_element_type=wide)]
    pallas_call x1, Pallas kernels: 78 us -> 74.5 us  [forward(): pl.pallas_call(functools.partial(forward_kernel, items, ring_size, depth,...]
    unnamed x48 -> x47, local copies, waits for them, and re-layouts: 5.78 us -> 5.72 us
where the time goes in v1:
time: 280 us; the launch traced here: 274 us
  Pallas kernels  210 us (75%)
  matrix products  31.9 us (11%)
  local copies, waits for them, and re-layouts  19.1 us (7%)
  other arithmetic  12.4 us (4%)
    pallas_call x1, Pallas kernels, backward(): pl.pallas_call(functools.partial(backward_kernel, items, ring_size, depth...  115 us
    pallas_call x1, Pallas kernels, forward(): pl.pallas_call(functools.partial(forward_kernel, items, ring_size, depth,...  74.5 us
    pallas_call x1, Pallas kernels, retrieve(): pl.pallas_call(functools.partial(retrieve_kernel, ring_size, dp_size), ou...  20.2 us
    dot_general x1, matrix products, fast_body(): jnp.dot(first_low, w_inner, preferred_element_type=wide) + b_inner  9.28 us
    dot_general x1, matrix products, fast_body(): jnp.einsum('nd,fd->nf', douter, w_outer, preferred_element_type=wide)  6.34 us
    unnamed x47, local copies, waits for them, and re-layouts  5.72 us

profile of v1, /device:TPU:0, one launch (start us, length us, event | category | flops | bytes accessed | tf_op | source)
XLA Modules:
  0.0 274.5 jit_solution(17913279950377453748)
XLA Ops:
  0.7 0.8 eq.16
  2.1 0.7 copy.66
  2.8 0.8 stack.55
  5.5 1.2 bitcast_convert_fusion.1
  6.7 74.5 %shard_map.347 = (bf16[768,1152]{1,0:T(8,128)(2,1)}, bf16[128,384]{1,0:T(8,128)(2,1)}, bf16[256,128]{1,0:T(8,128)(2,1)}, bf16[256,768]{1,0:T(8,128)(2,1)}, bf16[...) custom-call(bf16[96,768]{1,0:T(8,128)(2,1)} %refs_0_.1, ...), custom_call_target="tpu_custom_call" | custom-call | tf_op jit(solution)/shard_map/pallas_call | solution.py:852
  81.2 0.8 slice.77
  82.6 0.8 slice_convert_fusion
  83.4 0.7 slice.75
  85.2 2.5 fusion.14
  88.5 2.0 copy-done.10
  90.5 9.3 %fusion.5 = (bf16[512,3072]{1,0:T(8,128)(2,1)}, bf16[512,3072]{1,0:T(8,128)(2,1)S(1)}) fusion(f32[3072]{0:T(1024)S(1)} %bitcast.127, bf16[768,3072]{1,0:T(8,128)(2,1)S(1)} %copy-done.10, f32[512,768]{1,0:T(8,128)S(1)} %fusion.8, f32[768]{0:T(1024)S(1)} %add.148, f32[768]{0:T(1024)S(1)} %mul.123), kind=kOutput, calls=%fused_computation.7 | convolution fusion | flops 2457993216 | bytes 12601344 | tf_op jit(solution)/shard_map/dot_general | solution.py:1813
  99.8 2.7 fusion.25
  102.9 0.9 rsqrt.33.factor
  103.8 1.7 add_convert_fusion
  105.5 20.2 %shard_map.348 = (f32[2,256,768]{2,1,0:T(8,128)}, bf16[2,256,768]{2,1,0:T(8,128)(2,1)}, f32[8,768]{1,0:T(8,128)}, bf16[2,16,768]{2,1,0:T(8,128)(2,1)}, f32[2,16,128]{2,1,0:T(8,128)}, /*index=5*/f32[2,16,768]{2,1,0:T(8,128)}) custom-call(bf16[2,256,768]{2,1,0:T(8,128)(2,1)} %bitcast.111, bf16[2,256,768]{2,1,0:T(8,128)(2,1)} %bitcast.117, ...), custom_call_target="tpu_custom_call" | custom-call | tf_op jit(solution)/shard_map/pallas_call | solution.py:1629
  125.7 6.3 %convert_reduce_fusion = (f32[3072]{0:T(1024)S(1)}, bf16[512,3072]{1,0:T(8,128)(2,1)S(1)}) fusion(bf16[512,3072]{1,0:T(8,128)(2,1)} %get-tuple-element.61, bf16[512,768]{1,0:T(8,128)(2,1)} %bitcast.114, bf16[3072,768]{1,0:T(8,128)(2,1)} %get-tuple-element.52), kind=kOutput, calls=%fused_computation.8 | convolution fusion | flops 2423780352 | bytes 11808768 | tf_op jit(solution)/shard_map/nd,fd->nf/dot_general | solution.py:1837
  132.1 3.0 %multiply_reduce_fusion = (f32[768]{0:T(1024)S(1)}, f32[512]{0:T(512)S(1)}, f32[512]{0:T(512)S(1)}, f32[768]{0:T(1024)S(1)}, f32[512,768]{1,0:T(8,128)S(1)}) fusion(f32[512,768]{1,0:T(8,128)S(1)} %copy-done.2, f32[768]{0:T(1024)S(1)} %mul.123, bf16[512,3072]{1,0:T(8,128)(2,1)S(1)} %get-tuple-element.150, bf16[768,3072]{1,0:T(8,128)(2,1)S(1)} %bitcast.142, ...), kind=kOutput, calls=%fused_computation.19 | convolution fusion | flops 2419062272 | bytes 12596224 | tf_op jit(solution)/shard_map/nf,df->nd/dot_general | solution.py:1843
  136.0 0.8 slice_reduce_fusion.1
  136.8 0.7 unstack.35
  137.7 1.6 convert_reduce_fusion.1
  139.3 0.8 copy-done.15
  140.1 4.6 %convolution_convert_fusion.refs_11_ = bf16[768,3072]{1,0:T(8,128)(2,1)} fusion(bf16[512,3072]{1,0:T(8,128)(2,1)S(1)} %copy-done.15, f32[512,768]{1,0:T(8,128)S(1)} %copy-done.2, f32[768]{0:T(1024)S(1)} %add.148, f32[768]{0:T(1024)S(1)} %mul.123), kind=kOutput, calls=%fused_computation.11 | convolution fusion | flops 2419458048 | bytes 9443328 | tf_op jit(solution)/shard_map/nd,nf->df/dot_general | solution.py:1840
  144.7 1.7 fusion.10.refs_0_
  146.4 1.8 bitcast_convert_fusion.refs_12_
  148.4 0.7 pad.24
  149.1 115.0 %shard_map.349 = (bf16[2,256,768]{2,1,0:T(8,128)(2,1)}, bf16[384,768]{1,0:T(8,128)(2,1)}, bf16[96,3072]{1,0:T(8,128)(2,1)}, bf16[96,768]{1,0:T(8,128)(2,1)}, bf1...) custom-call(bf16[2,768,256]{2,1,0:T(8,128)(2,1)} %fusion.10.refs_0_, s32[1,1024]{1,0:T(1,128)} %dynamic-slice_bitcast_fusion.refs_1_, ...), custom_call_target="tpu_custom_call" | custom-call | tf_op jit(solution)/shard_map/pallas_call | solution.py:1473
  264.1 0.8 convert_element_type.115
  266.0 1.6 convert_element_type.114
  267.6 2.0 fusion.23
  269.7 1.1 convert_element_type.116
  270.8 1.1 convert_element_type.117
  273.2 0.9 copy.72
  (80 shorter events, 9.0 us)
Async XLA Ops:
  6.7 78.5 %copy-start = (bf16[2,1,256,768]{3,2,1,0:T(8,128)(2,1)S(1)}, bf16[2,1,256,768]{3,2,1,0:T(8,128)(2,1)}, u32[]{:S(2)}) copy-start(bf16[2,1,256,768]{3,2,1,0:T(8,128)(2,1)} %param.20) | copy-start | bytes 2359300
  88.2 2.3 copy-start.10
  88.2 11.6 %slice-start.2 = ((s8[4718592]{0:T(1024)(128)(4,1)}), s8[4194304]{0:T(1024)(128)(4,1)S(1)}, s32[]{:S(2)}) async-start(s8[4718592]{0:T(1024)(128)(4,1)} %bitcast.143), calls=%async_computation.2 | async-start | bytes 8388608
  90.5 9.3 %copy-start.1 = (f32[512,768]{1,0:T(8,128)}, f32[512,768]{1,0:T(8,128)S(1)}, u32[]{:S(2)}) copy-start(f32[512,768]{1,0:T(8,128)S(1)} %fusion.8) | copy-start | bytes 4718596
  90.5 9.3 %slice-start.3 = ((s8[4718592]{0:T(1024)(128)(4,1)}), s8[524288]{0:T(1024)(128)(4,1)S(1)}, s32[]{:S(2)}) async-start(s8[4718592]{0:T(1024)(128)(4,1)} %bitcast.143), calls=%async_computation.3 | async-start | bytes 1048576
  99.8 2.8 %copy-start.3 = (bf16[512,3072]{1,0:T(8,128)(2,1)}, bf16[512,3072]{1,0:T(8,128)(2,1)S(1)}, u32[]{:S(2)}) copy-start(bf16[512,3072]{1,0:T(8,128)(2,1)S(1)} %get-tuple-element.51.refs_9_) | copy-start | bytes 9437188
  105.5 26.6 %slice-start = ((s8[4718592]{0:T(1024)(128)(4,1)}), s8[524288]{0:T(1024)(128)(4,1)S(1)}, s32[]{:S(2)}) async-start(s8[4718592]{0:T(1024)(128)(4,1)} %bitcast.141), calls=%async_computation | async-start | bytes 1048576
  125.7 6.4 %copy-start.2 = (f32[512,768]{1,0:T(8,128)S(1)}, f32[512,768]{1,0:T(8,128)}, u32[]{:S(2)}) copy-start(f32[512,768]{1,0:T(8,128)} %copy-done.1) | copy-start | bytes 4718596
  125.7 6.4 %slice-start.1 = ((s8[4718592]{0:T(1024)(128)(4,1)}), s8[4194304]{0:T(1024)(128)(4,1)S(1)}, s32[]{:S(2)}) async-start(s8[4718592]{0:T(1024)(128)(4,1)} %bitcast.141), calls=%async_computation.1 | async-start | bytes 8388608
  125.7 6.4 %copy-start.11 = (f32[2,256,768]{2,1,0:T(8,128)S(1)}, f32[2,256,768]{2,1,0:T(8,128)}, u32[]{:S(2)}) copy-start(f32[2,256,768]{2,1,0:T(8,128)} %get-tuple-element.59) | copy-start | bytes 4718596
  132.1 3.1 %copy-start.14 = (bf16[512,3072]{1,0:T(8,128)(2,1)}, bf16[512,3072]{1,0:T(8,128)(2,1)S(1)}, u32[]{:S(2)}) copy-start(bf16[512,3072]{1,0:T(8,128)(2,1)S(1)} %get-tuple-element.150) | copy-start | bytes 9437188
  132.1 3.1 %copy-start.9 = (f32[2,16,128]{2,1,0:T(8,128)S(1)}, f32[2,16,128]{2,1,0:T(8,128)}, u32[]{:S(2)}) copy-start(f32[2,16,128]{2,1,0:T(8,128)} %get-tuple-element.57) | copy-start | bytes 49156
  137.7 2.5 copy-start.15
  140.1 4.6 %copy-start.12 = (bf16[768,768]{1,0:T(8,128)(2,1)S(1)}, bf16[768,768]{1,0:T(8,128)(2,1)}, u32[]{:S(2)}) copy-start(bf16[768,768]{1,0:T(8,128)(2,1)} %get-tuple-element.48) | copy-start | bytes 3538948
  144.7 1.7 copy-start.13
  264.1 5.6 %copy-start.6 = (bf16[96,3072]{1,0:T(8,128)(2,1)S(1)}, bf16[96,3072]{1,0:T(8,128)(2,1)}, u32[]{:S(2)}) copy-start(bf16[96,3072]{1,0:T(8,128)(2,1)} %get-tuple-element.72) | copy-start | bytes 1769476
  267.6 3.2 %copy-start.5 = (bf16[384,768]{1,0:T(8,128)(2,1)S(1)}, bf16[384,768]{1,0:T(8,128)(2,1)}, u32[]{:S(2)}) copy-start(bf16[384,768]{1,0:T(8,128)(2,1)} %get-tuple-element.73) | copy-start | bytes 1769476
  269.7 2.2 copy-start.8
  269.7 2.8 %copy-start.7 = (f32[2,16,768]{2,1,0:T(8,128)S(1)}, f32[2,16,768]{2,1,0:T(8,128)}, u32[]{:S(2)}) copy-start(f32[2,16,768]{2,1,0:T(8,128)} %get-tuple-element.176) | copy-start | bytes 294916
  269.7 3.5 %copy-start.4 = (bf16[2,256,768]{2,1,0:T(8,128)(2,1)S(1)}, bf16[2,256,768]{2,1,0:T(8,128)(2,1)}, u32[]{:S(2)}) copy-start(bf16[2,256,768]{2,1,0:T(8,128)(2,1)} %get-tuple-element.68) | copy-start | bytes 2359300

commit v2 on v1

--- a/solution.py
+++ b/solution.py
@@ -1239,6 +1239,7 @@
 
     loads[0].wait()
     loads[1].wait()
+    tick(2)
     for head in range(heads):
         if head + 2 < heads:
             send_head(head + 2)
@@ -1246,9 +1247,11 @@
         if head == 0:
             for copy in loads[5:]:
                 copy.wait()
-        if head < 4:
-            outer_work(2 * head)
-            outer_work(2 * head + 1)
+            for step in range(4):
+                outer_work(step)
+        if head in (1, 2):
+            outer_work(2 * head + 2)
+            outer_work(2 * head + 3)
         tick()
     loads[2].wait()
     loads[3].wait()
@@ -1610,7 +1613,7 @@
         dsecond[m] = inner_term
         rounded = inner_term.astype(jnp.bfloat16)
         douter[m] = rounded
-        for row, values in enumerate((product, dout, rounded.astype(jnp.float32))):
+        for row, values in enumerate((rounded.astype(jnp.float32), product, dout)):
             line = jnp.sum(values, axis=0, keepdims=True)
             if m == 0:
                 sums[row : row + 1] = line
@@ -1727,8 +1730,10 @@
         )
     )
     passages = dp_size * row_queries
-    hot = (
-        targets[:, :, None] == jnp.arange(passages, dtype=jnp.int32)[None, None, :]
+    hot = jnp.where(
+        targets.reshape(micro * row_queries, 1) == jnp.arange(passages, dtype=jnp.int32)[None],
+        1.0,
+        0.0,
     ).astype(narrow)
     seg_pack = jnp.pad(segment_ids.reshape(micro, block_tokens), ((0, 8 - micro), (0, 0)))
     shards = (
@@ -1736,7 +1741,7 @@
         key_weight,
         value_weight,
         pack,
-        hot.reshape(micro * row_queries, passages),
+        hot,
         queries.reshape(micro * row_queries, width),
         output_weight,
         inner_weight,
@@ -1800,6 +1805,7 @@
     seg_mine = lax.dynamic_slice(seg_row, (row_at, 0, 0), (1, 1, length)).reshape(1, length)
 
     flat_rows = hidden_in.reshape(tokens, width)
+    flat_rows, context_t = lax.optimization_barrier((flat_rows, context_t))
     attended = (
         jnp.einsum("met,ed->mtd", context_t, wo_full, preferred_element_type=wide).reshape(
             tokens, width
@@ -1833,7 +1839,6 @@
     query_loss = query_loss[:, :, 0]
     dsecond = dsecond.reshape(tokens, width)
     douter = douter.reshape(tokens, width)
-    gain_two_grad, shift_two_grad, outer_bias_grad = second_sums[:3]
     dactive = jnp.einsum("nd,fd->nf", douter, w_outer, preferred_element_type=wide)
     dinner = (dactive * slope.astype(wide)).astype(narrow)
     inner_bias_grad = jnp.sum(dinner.astype(wide), axis=0)
@@ -1853,16 +1858,11 @@
     dcontext_t = jnp.einsum(
         "mtd,ed->met", datt_rows, wo_full, preferred_element_type=wide
     ).astype(narrow)
-    vector_grads = jnp.stack(
+    vector_grads = jnp.concatenate(
         (
-            jnp.zeros((width,), wide),
-            jnp.zeros((width,), wide),
-            output_bias_grad,
-            gain_one_grad,
-            shift_one_grad,
-            outer_bias_grad,
-            gain_two_grad,
-            shift_two_grad,
+            jnp.zeros((2, width), wide),
+            jnp.stack((output_bias_grad, gain_one_grad, shift_one_grad)),
+            second_sums[:3],
         )
     )
     grad_pack = jnp.pad(

time: 280 us -> 275 us (0.982)
    unnamed x47 -> x43, local copies, waits for them, and re-layouts: 5.72 us -> 5.31 us
where the time goes in v2:
time: 275 us; the launch traced here: 270 us
  Pallas kernels  208 us (76%)
  matrix products  32.5 us (12%)
  local copies, waits for them, and re-layouts  17.2 us (6%)
  other arithmetic  11.1 us (4%)
    pallas_call x1, Pallas kernels, backward(): pl.pallas_call(functools.partial(backward_kernel, items, ring_size, depth...  113 us
    pallas_call x1, Pallas kernels, forward(): pl.pallas_call(functools.partial(forward_kernel, items, ring_size, depth,...  74.6 us
    pallas_call x1, Pallas kernels, retrieve(): pl.pallas_call(functools.partial(retrieve_kernel, ring_size, dp_size), ou...  20.1 us
    dot_general x1, matrix products, fast_body(): jnp.dot(first_low, w_inner, preferred_element_type=wide) + b_inner  9.35 us
    dot_general x1, matrix products, fast_body(): jnp.einsum('nd,fd->nf', douter, w_outer, preferred_element_type=wide)  6.34 us

profile of v2, /device:TPU:0, one launch (start us, length us, event | category | flops | bytes accessed | tf_op | source)
XLA Modules:
  0.0 270.1 jit_solution(14737200796681332275)
XLA Ops:
  0.7 0.8 eq.15
  1.4 0.7 broadcast_in_dim.12
  2.1 0.7 copy.60
  2.8 0.8 stack.38
  4.2 0.7 select_convert_fusion.refs_4_
  5.5 74.6 %shard_map.347 = (bf16[768,1152]{1,0:T(8,128)(2,1)}, bf16[128,384]{1,0:T(8,128)(2,1)}, bf16[256,128]{1,0:T(8,128)(2,1)}, bf16[256,768]{1,0:T(8,128)(2,1)}, bf16[...) custom-call(bf16[96,768]{1,0:T(8,128)(2,1)} %refs_0_.1, ...), custom_call_target="tpu_custom_call" | custom-call | tf_op jit(solution)/shard_map/pallas_call | solution.py:852
  80.1 0.8 slice.76
  81.5 0.8 slice_convert_fusion
  82.3 0.7 slice.74
  83.1 0.7 unstack.26.gain
  84.1 2.4 fusion.10
  87.1 1.7 copy-done.9
  88.8 9.4 %fusion.5 = (bf16[512,3072]{1,0:T(8,128)(2,1)}, bf16[512,3072]{1,0:T(8,128)(2,1)S(1)}) fusion(f32[3072]{0:T(1024)S(1)} %bitcast.100, bf16[768,3072]{1,0:T(8,128)(2,1)S(1)} %copy-done.9, f32[512,768]{1,0:T(8,128)S(1)} %get-tuple-element.128, f32[768]{0:T(1024)S(1)} %add.130, f32[768]{0:T(1024)S(1)} %mul.122, f32[512]{0:T(512)S(1)} %add_rsqrt_fusion.1, ...), kind=kOutput, calls=%fused_computation.7 | convolution fusion | flops 2458779648 | bytes 12605440 | tf_op jit(solution)/shard_map/dot_general | solution.py:1819
  98.2 2.8 %fusion.22 = (f32[512]{0:T(512)S(1)}, f32[512,768]{1,0:T(8,128)S(1)}) fusion(f32[768]{0:T(1024)S(1)} %add.145, bf16[512,3072]{1,0:T(8,128)(2,1)S(1)} %get-tuple-element.55.refs_9_, bf16[3072,768]{1,0:T(8,128)(2,1)S(1)} %bitcast.116, f32[768]{0:T(1024)S(1)} %add.130, f32[768]{0:T(1024)S(1)} %mul.122, f32[512]{0:T(512)S(1)} %add_rsqrt_fusion.1, ...), kind=kOutput, calls=%fused_computation.68 | convolution fusion | flops 2418671104 | bytes 11025408 | tf_op jit(solution)/shard_map/dot_general | solution.py:1822
  101.3 0.9 rsqrt.29.factor
  102.2 1.7 add_convert_fusion
  104.0 20.1 %shard_map.348 = (f32[2,256,768]{2,1,0:T(8,128)}, bf16[2,256,768]{2,1,0:T(8,128)(2,1)}, f32[8,768]{1,0:T(8,128)}, bf16[2,16,768]{2,1,0:T(8,128)(2,1)}, f32[2,16,128]{2,1,0:T(8,128)}, /*index=5*/f32[2,16,768]{2,1,0:T(8,128)}) custom-call(bf16[2,256,768]{2,1,0:T(8,128)(2,1)} %bitcast.87, bf16[2,256,768]{2,1,0:T(8,128)(2,1)} %bitcast.93, ...), custom_call_target="tpu_custom_call" | custom-call | tf_op jit(solution)/shard_map/pallas_call | solution.py:1632
  124.1 6.3 %convert_reduce_fusion = (f32[3072]{0:T(1024)S(1)}, bf16[512,3072]{1,0:T(8,128)(2,1)S(1)}) fusion(bf16[512,3072]{1,0:T(8,128)(2,1)} %get-tuple-element.65, bf16[512,768]{1,0:T(8,128)(2,1)} %bitcast.90, bf16[3072,768]{1,0:T(8,128)(2,1)} %get-tuple-element.56), kind=kOutput, calls=%fused_computation.8 | convolution fusion | flops 2423780352 | bytes 11808768 | tf_op jit(solution)/shard_map/nd,fd->nf/dot_general | solution.py:1842
  130.5 3.2 %multiply_reduce_fusion = (f32[768]{0:T(1024)S(1)}, f32[512]{0:T(512)S(1)}, f32[512]{0:T(512)S(1)}, f32[768]{0:T(1024)S(1)}, f32[512,768]{1,0:T(8,128)S(1)}) fusion(f32[512,768]{1,0:T(8,128)S(1)} %get-tuple-element.128, f32[512]{0:T(512)S(1)} %add_rsqrt_fusion.1, f32[512]{0:T(512)S(1)} %broadcast_multiply_fusion.3, f32[768]{0:T(1024)S(1)} %mul.122, ...), kind=kOutput, calls=%fused_computation.16 | convolution fusion | flops 2419848704 | bytes 12600320 | tf_op jit(solution)/shard_map/nf,df->nd/dot_general | solution.py:1848
  134.7 1.8 convert_reduce_fusion.1
  136.4 0.7 copy-done.14
  137.1 5.0 %convolution_convert_fusion.refs_11_ = bf16[768,3072]{1,0:T(8,128)(2,1)} fusion(bf16[512,3072]{1,0:T(8,128)(2,1)S(1)} %copy-done.14, f32[512,768]{1,0:T(8,128)S(1)} %get-tuple-element.128, f32[768]{0:T(1024)S(1)} %add.130, f32[768]{0:T(1024)S(1)} %mul.122, f32[512]{0:T(512)S(1)} %add_rsqrt_fusion.1, f32[512]{0:T(512)S(1)} %broadcast_multiply_fusion.3), kind=kOutput, calls=%fused_computation.11 | convolution fusion | flops 2420244480 | bytes 9447424 | tf_op jit(solution)/shard_map/nd,nf->df/dot_general | solution.py:1845
  142.2 1.7 fusion.8.refs_0_
  143.9 1.8 bitcast_convert_fusion.refs_12_
  145.8 0.7 pad.24
  146.5 113.1 %shard_map.349 = (bf16[2,256,768]{2,1,0:T(8,128)(2,1)}, bf16[384,768]{1,0:T(8,128)(2,1)}, bf16[96,3072]{1,0:T(8,128)(2,1)}, bf16[96,768]{1,0:T(8,128)(2,1)}, bf1...) custom-call(bf16[2,768,256]{2,1,0:T(8,128)(2,1)} %fusion.8.refs_0_, s32[1,1024]{1,0:T(1,128)} %dynamic-slice_bitcast_fusion.refs_1_, ...), custom_call_target="tpu_custom_call" | custom-call | tf_op jit(solution)/shard_map/pallas_call | solution.py:1476
  259.7 0.8 convert_element_type.105
  261.6 1.6 convert_element_type.104
  263.2 2.0 fusion.20
  265.3 1.1 convert_element_type.106
  266.4 1.1 convert_element_type.107
  268.8 0.9 copy.66
  (73 shorter events, 6.7 us)
Async XLA Ops:
  84.1 2.4 copy-start
  86.5 2.3 copy-start.9
  86.8 11.4 %slice-start.2 = ((s8[4718592]{0:T(1024)(128)(4,1)}), s8[4194304]{0:T(1024)(128)(4,1)S(1)}, s32[]{:S(2)}) async-start(s8[4718592]{0:T(1024)(128)(4,1)} %bitcast.115), calls=%async_computation.2 | async-start | bytes 8388608
  88.8 9.4 %slice-start.3 = ((s8[4718592]{0:T(1024)(128)(4,1)}), s8[524288]{0:T(1024)(128)(4,1)S(1)}, s32[]{:S(2)}) async-start(s8[4718592]{0:T(1024)(128)(4,1)} %bitcast.115), calls=%async_computation.3 | async-start | bytes 1048576
  98.2 2.8 %copy-start.1 = (bf16[512,3072]{1,0:T(8,128)(2,1)}, bf16[512,3072]{1,0:T(8,128)(2,1)S(1)}, u32[]{:S(2)}) copy-start(bf16[512,3072]{1,0:T(8,128)(2,1)S(1)} %get-tuple-element.55.refs_9_) | copy-start | bytes 9437188
  104.0 26.5 %slice-start = ((s8[4718592]{0:T(1024)(128)(4,1)}), s8[524288]{0:T(1024)(128)(4,1)S(1)}, s32[]{:S(2)}) async-start(s8[4718592]{0:T(1024)(128)(4,1)} %bitcast.113), calls=%async_computation | async-start | bytes 1048576
  124.1 6.4 %slice-start.1 = ((s8[4718592]{0:T(1024)(128)(4,1)}), s8[4194304]{0:T(1024)(128)(4,1)S(1)}, s32[]{:S(2)}) async-start(s8[4718592]{0:T(1024)(128)(4,1)} %bitcast.113), calls=%async_computation.1 | async-start | bytes 8388608
  124.1 6.4 %copy-start.10 = (f32[2,256,768]{2,1,0:T(8,128)S(1)}, f32[2,256,768]{2,1,0:T(8,128)}, u32[]{:S(2)}) copy-start(f32[2,256,768]{2,1,0:T(8,128)} %get-tuple-element.63) | copy-start | bytes 4718596
  130.5 3.3 %copy-start.13 = (bf16[512,3072]{1,0:T(8,128)(2,1)}, bf16[512,3072]{1,0:T(8,128)(2,1)S(1)}, u32[]{:S(2)}) copy-start(bf16[512,3072]{1,0:T(8,128)(2,1)S(1)} %get-tuple-element.152) | copy-start | bytes 9437188
  130.5 3.3 %copy-start.7 = (f32[2,16,128]{2,1,0:T(8,128)S(1)}, f32[2,16,128]{2,1,0:T(8,128)}, u32[]{:S(2)}) copy-start(f32[2,16,128]{2,1,0:T(8,128)} %get-tuple-element.61) | copy-start | bytes 49156
  130.5 4.0 %copy-start.8 = (f32[8,768]{1,0:T(8,128)S(1)}, f32[8,768]{1,0:T(8,128)}, u32[]{:S(2)}) copy-start(f32[8,768]{1,0:T(8,128)} %get-tuple-element.66) | copy-start | bytes 73732
  134.7 2.5 copy-start.14
  137.1 5.0 %copy-start.11 = (bf16[768,768]{1,0:T(8,128)(2,1)S(1)}, bf16[768,768]{1,0:T(8,128)(2,1)}, u32[]{:S(2)}) copy-start(bf16[768,768]{1,0:T(8,128)(2,1)} %get-tuple-element.52) | copy-start | bytes 3538948
  142.2 1.7 copy-start.12
  259.7 5.6 %copy-start.4 = (bf16[96,3072]{1,0:T(8,128)(2,1)S(1)}, bf16[96,3072]{1,0:T(8,128)(2,1)}, u32[]{:S(2)}) copy-start(bf16[96,3072]{1,0:T(8,128)(2,1)} %get-tuple-element.76) | copy-start | bytes 1769476
  263.2 3.2 %copy-start.3 = (bf16[384,768]{1,0:T(8,128)(2,1)S(1)}, bf16[384,768]{1,0:T(8,128)(2,1)}, u32[]{:S(2)}) copy-start(bf16[384,768]{1,0:T(8,128)(2,1)} %get-tuple-element.77) | copy-start | bytes 1769476
  265.3 2.2 copy-start.6
  265.3 2.8 %copy-start.5 = (f32[2,16,768]{2,1,0:T(8,128)S(1)}, f32[2,16,768]{2,1,0:T(8,128)}, u32[]{:S(2)}) copy-start(f32[2,16,768]{2,1,0:T(8,128)} %get-tuple-element.178) | copy-start | bytes 294916
  265.3 3.5 %copy-start.2 = (bf16[2,256,768]{2,1,0:T(8,128)(2,1)S(1)}, bf16[2,256,768]{2,1,0:T(8,128)(2,1)}, u32[]{:S(2)}) copy-start(bf16[2,256,768]{2,1,0:T(8,128)(2,1)} %get-tuple-element.72) | copy-start | bytes 2359300
